TPU v7x, 512 devices: a whole 4x4x16 slice. The times are simulated.
512 devices in a mesh: lat: 16 (over z_lo, core), lon: 32 (over z_hi, y, x).
Axes of the slice: x: 4, y: 4, z: 16 (z_hi: 2, z_lo: 8; z = z_hi * 8 + z_lo), core: 2. Of those that a mesh axis runs over, the one named last changes fastest.
Arguments:
- inputs: bfloat16 [128, 512, 256], P('lat', 'lon'), may hold values from -6 to 6
- out_grad: bfloat16 [128, 512, 256], P('lat', 'lon'), may hold values from -6 to 6
- weight: bfloat16 [9, 256, 256], replicated, may hold values from -0.125 to 0.125
- kernel_basis: bfloat16 [128, 9, 17, 33], P('lat'), may hold values from -0.25 to 0.25
- band_start: int32 [128], P('lat'), may hold values from 0 to 8, as said below
- band_width: int32 [128], P('lat'), may hold values from 1 to 17
- lon_reach: int32 [128], P('lat'), may hold values from 1 to 16
Outputs:
- output: bfloat16 [128, 512, 256], P('lat', 'lon')
- input_grad: bfloat16 [128, 512, 256], P('lat', 'lon')
- weight_grad: float32 [9, 256, 256], replicated
Inputs may be any that keep to these rules, and one draw needn't show every extreme that they name: band_start + band_width <= 17 on every row.
All inputs are finite; a program needn't handle non-finite values.
Results may differ from a plain program's by a relative error of at most 0.0049.
Values may be sent and summed in bfloat16 or wider, within the bound.
A program may use at most 64 MiB of HBM per device.

v0:
```python
import math

import jax
import jax.numpy as jnp
from jax import lax
from jax.sharding import PartitionSpec as P


def extended_2(cells, sides, width, closed):
    for axis, dim in sides:
        count = lax.axis_size(axis)
        ends = count if closed else count - 1
        head = lax.slice_in_dim(cells, 0, width, axis=dim)
        tail = lax.slice_in_dim(cells, cells.shape[dim] - width, cells.shape[dim], axis=dim)
        cells = jnp.concatenate(
            [
                lax.ppermute(tail, axis, [(i, (i + 1) % count) for i in range(ends)]),
                cells,
                lax.ppermute(head, axis, [((i + 1) % count, i) for i in range(ends)]),
            ],
            axis=dim,
        )
    return cells


def keep_basis(kernel_basis, band_start, band_width, lon_reach):
    band_size = kernel_basis.shape[2]
    lon_size = kernel_basis.shape[3]
    lon_middle = (lon_size - 1) // 2
    band_pos = jnp.arange(band_size, dtype=jnp.int32)[None, :, None]
    lon_pos = jnp.arange(lon_size, dtype=jnp.int32)[None, None, :]
    starts = band_start[:, None, None]
    inside = (band_pos >= starts) & (band_pos < starts + band_width[:, None, None])
    inside = inside & (jnp.abs(lon_pos - lon_middle) <= lon_reach[:, None, None])
    return jnp.where(inside[:, None], kernel_basis, jnp.zeros_like(kernel_basis))


def forward_operator(kept, basis_index, columns):
    rows_here, basis_count, band_size, lon_size = kept.shape
    ext_rows = rows_here + band_size - 1
    ext_cols = columns + lon_size - 1
    chosen = lax.dynamic_index_in_dim(kept, basis_index, 1, keepdims=False)
    col_pick = (
        jnp.arange(ext_cols)[None, :, None] - jnp.arange(columns)[:, None, None]
        == jnp.arange(lon_size)[None, None, :]
    ).astype(jnp.bfloat16)
    row_pick = (
        jnp.arange(ext_rows)[None, :, None] - jnp.arange(rows_here)[:, None, None]
        == jnp.arange(band_size)[None, None, :]
    ).astype(jnp.bfloat16)
    spread = jnp.einsum(
        "ibd,jmd->ibjm", chosen, col_pick, preferred_element_type=jnp.float32
    ).astype(jnp.bfloat16)
    placed = jnp.einsum(
        "ibjm,ieb->ijem", spread, row_pick, preferred_element_type=jnp.float32
    ).astype(jnp.bfloat16)
    return placed.reshape(rows_here * columns, ext_rows * ext_cols)


def on_device(inputs, out_grad, weight, kernel_basis, band_start, band_width, lon_reach):
    rows_here, columns, channels = inputs.shape
    kept = keep_basis(kernel_basis, band_start, band_width, lon_reach)
    basis_count, band_size, lon_size = (kept.shape[1], kept.shape[2], kept.shape[3])
    lat_reach = (band_size - 1) // 2
    lon_half = (lon_size - 1) // 2
    ext_rows = rows_here + 2 * lat_reach
    ext_cols = columns + 2 * lon_half
    basis_ids = jnp.arange(basis_count, dtype=jnp.int32)
    extended = extended_2(inputs, (("lat", 0),), lat_reach, False)
    extended = extended_2(extended, (("lon", 1),), lon_half, True)
    flat_input = extended.reshape(ext_rows * ext_cols, channels)

    def contract(basis_index):
        operator = forward_operator(kept, basis_index, columns)
        return jnp.dot(operator, flat_input, preferred_element_type=jnp.float32).astype(
            jnp.bfloat16
        )

    mixed_in = lax.map(contract, basis_ids)
    grad_flat = out_grad.reshape(rows_here * columns, channels)
    output = jnp.einsum("kpc,koc->po", mixed_in, weight, preferred_element_type=jnp.float32)
    output = output.astype(jnp.bfloat16).reshape(rows_here, columns, channels)
    grad_scale = 1.0 / math.sqrt(rows_here * columns * lax.axis_size("lat") * lax.axis_size("lon"))
    local_grad = (
        jnp.einsum("po,kpc->koc", grad_flat, mixed_in, preferred_element_type=jnp.float32)
        * grad_scale
    )
    weight_grad = lax.psum(local_grad, ("lat", "lon"))
    mixed_grad = jnp.einsum(
        "po,koc->kpc", grad_flat, weight, preferred_element_type=jnp.float32
    ).astype(jnp.bfloat16)

    def return_step(running, basis_index):
        operator = forward_operator(kept, basis_index, columns)
        contrib = lax.dot_general(
            operator,
            mixed_grad[basis_index],
            (((0,), (0,)), ((), ())),
            preferred_element_type=jnp.float32,
        )
        return (running + contrib, None)

    padded_grad, unused = lax.scan(
        return_step, jnp.zeros((ext_rows * ext_cols, channels), jnp.float32), basis_ids
    )
    padded_grad = padded_grad.reshape(ext_rows, ext_cols, channels)
    side_rims = extended_2(padded_grad, (("lon", 1),), lon_half, True)
    lat_part = padded_grad[:, lon_half : lon_half + columns]
    lat_part = lat_part.at[:, :lon_half].add(side_rims[:, :lon_half])
    lat_part = lat_part.at[:, columns - lon_half :].add(side_rims[:, ext_cols + lon_half :])
    lat_rims = extended_2(lat_part, (("lat", 0),), lat_reach, False)
    input_grad = lat_part[lat_reach : lat_reach + rows_here]
    input_grad = input_grad.at[:lat_reach].add(lat_rims[:lat_reach])
    input_grad = input_grad.at[rows_here - lat_reach :].add(lat_rims[ext_rows + lat_reach :])
    return (output, input_grad.astype(jnp.bfloat16), weight_grad)


def solution(mesh):
    placed = (
        P("lat", "lon", None),
        P("lat", "lon", None),
        P(),
        P("lat", None, None, None),
        P("lat"),
        P("lat"),
        P("lat"),
    )
    return jax.shard_map(
        on_device,
        mesh=mesh,
        in_specs=placed,
        out_specs=(P("lat", "lon", None), P("lat", "lon", None), P()),
        check_vma=False,
    )
```

profile of v0, /device:TPU:1, one launch (start us, length us, event | category | flops | bytes accessed | tf_op | source)
XLA Modules:
  0.0 695.4 jit_solution(2958693216303774192)
XLA Ops:
  7.2 5.1 collective-permute-start
  12.3 5.7 collective-permute-start.1
  18.1 0.7 add.65
  18.8 0.7 fusion.40
  19.5 0.7 broadcast_compare_fusion
  20.3 1.8 copy_select_fusion
  22.1 2.2 fusion.35
  24.3 55.9 %while.30 = (s32[]{:T(128)}, f32[1152,256]{1,0:T(8,128)S(1)}, s32[9]{0:T(128)S(1)}, bf16[8,9,17,33]{3,2,1,0:T(8,128)(2,1)}, bf16[9,128,256]{1,2,0:T(8,128)(2,1)}, /*index=5*/s32[]{:T(128)}, s32[]{:T(128)}, s32[]{:T(128)}) while((s32[]{:T(128)}, f32[1152,256]{1,0:T(8,128)S(1)}, s32[9]{0:T(128)S(1)}, ...), condition=%wide.region_3.4_spmd.clone, body=%wide.region_2.3_spmd.clone.sunk | while | flops 88275848 | bytes 3661469 | solution.py:103
  26.8 1.6 fusion.77
  29.0 1.5 convolution_add_fusion.2
  33.1 1.6 fusion.77
  35.2 1.5 convolution_add_fusion.2
  36.7 0.6 dynamic_slice.43
  39.3 1.6 fusion.77
  41.4 1.5 convolution_add_fusion.2
  45.5 1.6 fusion.77
  47.7 1.5 convolution_add_fusion.2
  51.7 1.6 fusion.77
  53.9 1.5 convolution_add_fusion.2
  57.9 1.6 fusion.77
  60.1 1.5 convolution_add_fusion.2
  64.2 1.6 fusion.77
  66.3 1.5 convolution_add_fusion.2
  70.4 1.6 fusion.77
  72.5 1.5 convolution_add_fusion.2
  76.6 1.6 fusion.77
  78.8 1.5 convolution_add_fusion.2
  80.3 0.8 constant_dynamic-update-slice_fusion.2
  81.1 0.8 constant_dynamic-update-slice_fusion
  82.0 15.3 %collective-permute-start.3 = (bf16[24,16,256]{2,1,0:T(8,128)(2,1)S(1)}, bf16[24,16,256]{2,1,0:T(8,128)(2,1)S(1)}, u32[]{:S(2)}, u32[]{:S(2)}) collective-permute-start(bf16[24,16,256]{2,1,0:T(8,128)(2,1)S(1)} %constant_dynamic-update-slice_fusion), channel_id=1, source_target_pairs={{1,0},{2,1},{3,2},{4,3},{5,4},{6,5},{7,6},{8,7},{9,8},{10,9},{11,1... | collective-permute-start | bytes 589832 | tf_op jit(solution)/shard_map/ppermute | solution.py:19
  97.3 1.9 collective-permute-start.2
  99.2 0.9 fusion.41
  100.2 1.9 collective-permute-start.4
  102.1 16.3 %collective-permute-start.5 = (f32[24,16,256]{2,1,0:T(8,128)}, f32[24,16,256]{2,1,0:T(8,128)}, u32[]{:S(2)}, u32[]{:S(2)}) collective-permute-start(f32[24,16,256]{2,1,0:T(8,128)} %get-tuple-element.186), channel_id=1, source_target_pairs={{1,0},{2,1},{3,2},{4,3},{5,4},{6,5},{7,6},{8,7},{9,8},{10,9},{11,1... | collective-permute-start | bytes 1179656 | tf_op jit(solution)/shard_map/ppermute | solution.py:19
  118.4 0.9 collective-permute-done.2
  119.3 0.9 pad_maximum_fusion
  120.1 59.9 %while.29 = (s32[]{:T(128)}, bf16[9,128,256]{2,1,0:T(8,128)(2,1)}, s32[9]{0:T(128)S(1)}, bf16[8,9,17,33]{3,2,1,0:T(8,128)(2,1)}, bf16[1152,256]{1,0:T(8,128)(2,1)}, /*index=5*/s32[]{:T(128)}, s32[]{:T(128)}, s32[]{:T(128)}) while((s32[]{:T(128)}, bf16[9,128,256]{2,1,0:T(8,128)(2,1)}, s32[9]{0:T(128)S(1)}, bf16[8,9,17,33]{3,2,1,0:T(8,128)(2,1)}, ...), condition=%wide.region_1.2_spmd, body=%wide.region_0.1_spmd.sunk | while | flops 87718784 | bytes 1891987 | solution.py:79
  122.7 1.6 fusion.70
  124.8 2.0 fusion.71
  129.3 1.6 fusion.70
  131.5 2.0 fusion.71
  136.0 1.6 fusion.70
  138.2 2.0 fusion.71
  142.7 1.6 fusion.70
  144.8 2.0 fusion.71
  149.3 1.6 fusion.70
  151.5 1.9 fusion.71
  156.0 1.6 fusion.70
  158.1 1.9 fusion.71
  162.6 1.6 fusion.70
  164.8 2.0 fusion.71
  169.3 1.6 fusion.70
  171.4 2.0 fusion.71
  175.9 1.6 fusion.70
  178.1 2.0 fusion.71
  180.0 3.0 multiply_bitcast_fusion
  183.1 1.3 fusion.37
  184.4 21.9 %collective-permute-start.6 = (f32[8,16,256]{2,1,0:T(8,128)S(1)}, f32[8,16,256]{2,1,0:T(8,128)S(1)}, u32[]{:S(2)}, u32[]{:S(2)}) collective-permute-start(f32[8,16,256]{2,1,0:T(8,128)S(1)} %get-tuple-element.187), channel_id=1, source_target_pairs={{0,32},{32,64},{64,96},{96,128},{128,160},{160,192},{192,224},{224... | collective-permute-start | bytes 393224 | tf_op jit(solution)/shard_map/ppermute | solution.py:17
  206.2 1.9 collective-permute-start.7
  208.2 1.2 fusion.36
  209.4 3.2 collective-permute-done.7
  212.5 0.7 fusion.39
  213.2 472.3 %all-reduce.2.cloned.1.call-done = f32[9,256,256]{1,2,0:T(8,128)} async-done(((f32[9,256,256]{1,2,0:T(8,128)}), f32[9,256,256]{1,2,0:T(8,128)}) %all-reduce.2.cloned.1.call-update) | async-done | bytes 2359312 | tf_op jit(solution)/shard_map/psum | solution.py:88
  685.5 3.0 copy.14
  (95 shorter events, 19.9 us)
Async XLA Ops:
  7.2 15.0 %copy-start = (bf16[9,256,256]{2,1,0:T(8,128)(2,1)S(1)}, bf16[9,256,256]{2,1,0:T(8,128)(2,1)}, u32[]{:S(2)}) copy-start(bf16[9,256,256]{2,1,0:T(8,128)(2,1)} %param.29) | copy-start | bytes 3538948
  7.2 678.3 %all-reduce.2.cloned.1.call-start = ((), (), s32[]{:S(2)}) async-start(), calls=%async_computation | async-start | bytes 4718592 | tf_op jit(solution)/shard_map/psum | solution.py:88
  7.2 73.0 %collective-permute-start = (bf16[8,16,256]{2,1,0:T(8,128)(2,1)}, bf16[8,16,256]{2,1,0:T(8,128)(2,1)}, u32[]{:S(2)}, u32[]{:S(2)}) collective-permute-start(bf16[8,16,256]{2,1,0:T(8,128)(2,1)} %param.27), channel_id=1, source_target_pairs={{0,32},{32,64},{64,96},{96,128},{128,160},{160,192},{192,224},{224... | collective-permute-start | bytes 196616 | tf_op jit(solution)/shard_map/ppermute | solution.py:17
  12.3 68.8 %collective-permute-start.1 = (bf16[8,16,256]{2,1,0:T(8,128)(2,1)}, bf16[8,16,256]{2,1,0:T(8,128)(2,1)}, u32[]{:S(2)}, u32[]{:S(2)}) collective-permute-start(bf16[8,16,256]{2,1,0:T(8,128)(2,1)} %param.27), channel_id=1, source_target_pairs={{32,0},{64,32},{96,64},{128,96},{160,128},{192,160},{224,192},{256... | collective-permute-start | bytes 196616 | tf_op jit(solution)/shard_map/ppermute | solution.py:19
  24.3 56.8 %copy-start.3 = (bf16[8,16,256]{2,1,0:T(8,128)(2,1)S(1)}, bf16[8,16,256]{2,1,0:T(8,128)(2,1)}, u32[]{:S(2)}) copy-start(bf16[8,16,256]{2,1,0:T(8,128)(2,1)} %param.27) | copy-start | bytes 196612
  82.0 36.4 %collective-permute-start.3 = (bf16[24,16,256]{2,1,0:T(8,128)(2,1)S(1)}, bf16[24,16,256]{2,1,0:T(8,128)(2,1)S(1)}, u32[]{:S(2)}, u32[]{:S(2)}) collective-permute-start(bf16[24,16,256]{2,1,0:T(8,128)(2,1)S(1)} %constant_dynamic-update-slice_fusion), channel_id=1, source_target_pairs={{1,0},{2,1},{3,2},{4,3},{5,4},{6,5},{7,6},{8,7},{9,8},{10,9},{11,1... | collective-permute-start | bytes 589832 | tf_op jit(solution)/shard_map/ppermute | solution.py:19
  97.3 22.0 %collective-permute-start.2 = (bf16[24,16,256]{2,1,0:T(8,128)(2,1)S(1)}, bf16[24,16,256]{2,1,0:T(8,128)(2,1)S(1)}, u32[]{:S(2)}, u32[]{:S(2)}) collective-permute-start(bf16[24,16,256]{2,1,0:T(8,128)(2,1)S(1)} %constant_dynamic-update-slice_fusion), channel_id=1, source_target_pairs={{0,1},{1,2},{2,3},{3,4},{4,5},{5,6},{6,7},{7,8},{8,9},{9,10},{10,1... | collective-permute-start | bytes 589832 | tf_op jit(solution)/shard_map/ppermute | solution.py:17
  100.2 82.9 %collective-permute-start.4 = (f32[24,16,256]{2,1,0:T(8,128)}, f32[24,16,256]{2,1,0:T(8,128)}, u32[]{:S(2)}, u32[]{:S(2)}) collective-permute-start(f32[24,16,256]{2,1,0:T(8,128)} %get-tuple-element.185), channel_id=1, source_target_pairs={{0,1},{1,2},{2,3},{3,4},{4,5},{5,6},{6,7},{7,8},{8,9},{9,10},{10,1... | collective-permute-start | bytes 1179656 | tf_op jit(solution)/shard_map/ppermute | solution.py:17
  102.1 81.0 %collective-permute-start.5 = (f32[24,16,256]{2,1,0:T(8,128)}, f32[24,16,256]{2,1,0:T(8,128)}, u32[]{:S(2)}, u32[]{:S(2)}) collective-permute-start(f32[24,16,256]{2,1,0:T(8,128)} %get-tuple-element.186), channel_id=1, source_target_pairs={{1,0},{2,1},{3,2},{4,3},{5,4},{6,5},{7,6},{8,7},{9,8},{10,9},{11,1... | collective-permute-start | bytes 1179656 | tf_op jit(solution)/shard_map/ppermute | solution.py:19
  120.1 59.9 %copy-start.2 = (bf16[8,16,256]{2,1,0:T(8,128)(2,1)S(1)}, bf16[8,16,256]{2,1,0:T(8,128)(2,1)}, u32[]{:S(2)}) copy-start(bf16[8,16,256]{2,1,0:T(8,128)(2,1)} %param.28) | copy-start | bytes 196612
  183.0 25.1 %copy-start.1 = (bf16[9,128,256]{2,1,0:T(8,128)(2,1)S(1)}, bf16[9,128,256]{2,1,0:T(8,128)(2,1)}, u32[]{:S(2)}) copy-start(bf16[9,128,256]{2,1,0:T(8,128)(2,1)} %get-tuple-element.137) | copy-start | bytes 1769476
  184.4 25.0 %collective-permute-start.6 = (f32[8,16,256]{2,1,0:T(8,128)S(1)}, f32[8,16,256]{2,1,0:T(8,128)S(1)}, u32[]{:S(2)}, u32[]{:S(2)}) collective-permute-start(f32[8,16,256]{2,1,0:T(8,128)S(1)} %get-tuple-element.187), channel_id=1, source_target_pairs={{0,32},{32,64},{64,96},{96,128},{128,160},{160,192},{192,224},{224... | collective-permute-start | bytes 393224 | tf_op jit(solution)/shard_map/ppermute | solution.py:17
  206.2 6.3 collective-permute-start.7
Sparse Core Ops, SparseCore 0:
  183.2 502.2 all-reduce.1
where the time goes:
time: 699 us; the launch traced here: 695 us
  waiting for transfers between devices  476 us (68%)
  starting transfers between devices  70.1 us (10%)
  matrix products  66.2 us (9%)
  loops' own time  35.7 us (5%)
  local copies, waits for them, and re-layouts  25.8 us (4%)
  between operations  14.2 us (2%)
  other arithmetic  7.01 us (1%)
    psum x1, waiting for transfers between devices, on_device(): weight_grad = lax.psum(local_grad, ('lat', 'lon'))  472 us
    ppermute x4, starting transfers between devices, extended_2(): lax.ppermute(head, axis, [((i + 1) % count, i) for i in range(ends)])  39.3 us
    ppermute x4, starting transfers between devices, extended_2(): lax.ppermute(tail, axis, [(i, (i + 1) % count) for i in range(ends)])  30.8 us
    dot_general x18, matrix products, forward_operator(): jnp.einsum('ibjm,ieb->ijem', spread, row_pick, preferred_element_type=jnp...  28.9 us
    another operation x1, loops' own time, on_device(): lax.scan(return_step, jnp.zeros((ext_rows * ext_cols, channels), jnp.floa...  17.9 us
    another operation x1, loops' own time, on_device(): mixed_in = lax.map(contract, basis_ids)  17.7 us
    dot_general x9, matrix products, contract(): jnp.dot(operator, flat_input, preferred_element_type=jnp.float32)  17.6 us
  transfers between devices with their start and end apart: 9, of which 3 were waited for; matrix products, arithmetic and copies ran while one was open for 14% of the time, Pallas kernels for 0%

commit v1 on v0

v1 whole, which is shorter than its diff:
```python
import functools
import math

import jax
import jax.numpy as jnp
from jax import lax
from jax.experimental import pallas as pl
from jax.experimental.pallas import tpu as pltpu
from jax.sharding import PartitionSpec as P

MESH = pl.DeviceIdType.MESH
F32, BF16 = jnp.float32, jnp.bfloat16

ROWS, COLS, CH = 8, 16, 256
CELLS = ROWS * COLS
K, BAND, LONW = 9, 17, 33
EXT = 3 * ROWS
PITCH = 64
FLAT = EXT * PITCH
PAIRS = EXT // 2
HALF = 128
GROUPS = 3
KG = K // GROUPS
SLICE = 16


def whole_wait(buf, sem):
    pltpu.make_async_copy(buf, buf, sem).wait()


def kernel(
    x_ref, g_ref, w_ref, kb_ref, start_ref, width_ref, reach_ref,
    out_ref, ig_ref, dw_ref,
    xh, kbs, comb, op, mg, mgt, mid, lat_out, lat_in, lon_out, lon_in,
    gt, gpeer, mfull, mm, msend, dws, rsb, zs, zb, zg, zgd, fin, dwv,
    xsend, xrecv, gsem, igsend, igrecv, msem_s, msem_r,
    rs_s, rs_r, z_s, z_r, zg_s, zg_r, fin_s, fin_r, ag_s, ag_r, fw_s, fw_r, loc,
):
    lat, lon = lax.axis_index("lat"), lax.axis_index("lon")
    core = lax.rem(lat, 2)
    zlo = lat // 2
    zhi = lon // 16
    rank = lax.rem(lon, 16)
    z4 = lax.rem(zlo, 4)
    zgroup = zhi * 2 + zlo // 4
    up, down = lat - 1, lat + 1
    has_up, has_down = lat > 0, lat < 15
    east, west = lax.rem(lon + 1, 32), lax.rem(lon + 31, 32)
    partner = (lat + 1 - 2 * core, lon)

    def plane_peer(d):
        return (lat, zhi * 16 + lax.rem(rank + d, 16))

    def z4_peer(t):
        return ((zlo - z4 + t) * 2 + core, lon)

    def zfar_peer(t):
        return (((t % 2) * 4 + z4) * 2 + core, (t // 2) * 16 + rank)

    def remote(src, dst, ssem, rsem, dev):
        return pltpu.make_async_remote_copy(
            src_ref=src, dst_ref=dst, send_sem=ssem, recv_sem=rsem, device_id=dev, device_id_type=MESH
        )

    xh[...] = jnp.zeros_like(xh)
    lat_in[...] = jnp.zeros_like(lat_in)

    bar = pltpu.get_barrier_semaphore()

    def signal(dev):
        pl.semaphore_signal(bar, inc=1, device_id=dev, device_id_type=MESH)

    signal((lat, east))
    signal((lat, west))
    for d in range(1, 4):
        signal(zfar_peer(lax.rem(zgroup + d, 4)))
    for d in range(1, 16):
        signal(plane_peer(d))
    for d in range(1, 4):
        signal(z4_peer(lax.rem(z4 + d, 4)))

    @pl.when(has_up)
    def _():
        signal((up, lon))

    @pl.when(has_down)
    def _():
        signal((down, lon))

    kbs[...] = jnp.zeros_like(kbs)
    band_pos = lax.broadcasted_iota(jnp.int32, (BAND, LONW), 0)
    lon_off = jnp.abs(lax.broadcasted_iota(jnp.int32, (BAND, LONW), 1) - (LONW - 1) // 2)

    xh[ROWS : 2 * ROWS, COLS : 2 * COLS, :] = x_ref[...]

    def op_step(k, carry):
        for i in range(ROWS):
            first = start_ref[i]
            inside = (band_pos >= first) & (band_pos < first + width_ref[i]) & (lon_off <= reach_ref[i])
            kbs[i, 1 : 1 + BAND, 0:LONW] = jnp.where(inside, kb_ref[i, k].astype(F32), 0.0)
            comb[i] = kbs[i, 0:24] + pltpu.roll(kbs[i, 1:25], PITCH, 1)
        for i in range(ROWS):
            for q in range(PAIRS):
                t = 2 * q - i + 1
                if 0 <= t <= BAND:
                    row = jnp.broadcast_to(comb[i, t : t + 1, :], (COLS, 128))
                    tile = pltpu.roll(row, 0, 1, stride=1, stride_axis=0)
                    op[k, i * COLS : (i + 1) * COLS, q * 128 : (q + 1) * 128] = tile.astype(BF16)
                else:
                    op[k, i * COLS : (i + 1) * COLS, q * 128 : (q + 1) * 128] = jnp.zeros((COLS, 128), BF16)
        return carry

    lax.fori_loop(0, K, op_step, 0)

    g = g_ref[...].reshape(CELLS, CH)

    def mg_step(k, carry):
        part = jnp.dot(g, w_ref[k], preferred_element_type=F32).astype(BF16)
        mg[k] = part.astype(F32).T.astype(BF16)
        return carry

    lax.fori_loop(0, K, mg_step, 0)
    for k in range(K):
        mgt[:, k * CELLS : (k + 1) * CELLS] = mg[k]
    gt[:, 0:CELLS] = g.astype(F32).T.astype(BF16)

    for n in range(FLAT // 256):
        part = jnp.dot(
            mgt[...], op[:, :, n * 256 : (n + 1) * 256].reshape(K * CELLS, 256), preferred_element_type=F32
        )
        part = part.T.reshape(4, PITCH, CH)[:, : 3 * COLS]
        r = n * 4
        if r < ROWS:
            lat_out[0, r : r + 4] = part.astype(BF16)
        elif r < 2 * ROWS:
            mid[r - ROWS : r - ROWS + 4] = part
        else:
            lat_out[1, r - 2 * ROWS : r - 2 * ROWS + 4] = part.astype(BF16)

    pl.semaphore_wait(bar, 23 + has_up.astype(jnp.int32) + has_down.astype(jnp.int32))

    mid_rows, top, bottom = pl.ds(ROWS, ROWS), pl.ds(0, ROWS), pl.ds(2 * ROWS, ROWS)
    mid_cols, wcols, ecols = pl.ds(COLS, COLS), pl.ds(0, COLS), pl.ds(2 * COLS, COLS)
    to_east = remote(x_ref, xh.at[mid_rows, wcols], xsend.at[0], xrecv.at[0], (lat, east))
    to_west = remote(x_ref, xh.at[mid_rows, ecols], xsend.at[1], xrecv.at[1], (lat, west))
    to_east.start()
    to_west.start()
    g_send = remote(g_ref, gpeer, gsem.at[0], gsem.at[1], partner)
    g_send.start()

    def up_down(cols, s):
        src = xh.at[mid_rows, cols]
        return (
            remote(src, xh.at[bottom, cols], xsend.at[s], xrecv.at[s], (up, lon)),
            remote(src, xh.at[top, cols], xsend.at[s + 1], xrecv.at[s + 1], (down, lon)),
        )

    verticals = (up_down(mid_cols, 2), up_down(wcols, 4), up_down(ecols, 6))
    ig_up = remote(lat_out.at[0], lat_in.at[1], igsend.at[0], igrecv.at[0], (up, lon))
    ig_down = remote(lat_out.at[1], lat_in.at[0], igsend.at[1], igrecv.at[1], (down, lon))

    def start_vertical(pair):
        @pl.when(has_up)
        def _():
            pair[0].start()

        @pl.when(has_down)
        def _():
            pair[1].start()

    def wait_vertical(pair):
        @pl.when(has_down)
        def _():
            pair[0].wait_recv()

        @pl.when(has_up)
        def _():
            pair[1].wait_recv()

    start_vertical(verticals[0])
    start_vertical((ig_up, ig_down))

    g_send.wait_recv()
    gt[:, CELLS : 2 * CELLS] = gpeer[...].reshape(CELLS, CH).astype(F32).T.astype(BF16)
    wait_vertical((ig_up, ig_down))
    total = mid[...] + lat_in[0].astype(F32) + lat_in[1].astype(F32)
    lon_out[0] = total[:, 0:COLS].astype(BF16)
    lon_out[1] = total[:, 2 * COLS : 3 * COLS].astype(BF16)
    mid[:, COLS : 2 * COLS] = total[:, COLS : 2 * COLS]
    ig_west = remote(lon_out.at[0], lon_in.at[1], igsend.at[2], igrecv.at[2], (lat, west))
    ig_east = remote(lon_out.at[1], lon_in.at[0], igsend.at[3], igrecv.at[3], (lat, east))

    to_east.wait_recv()
    start_vertical(verticals[1])
    to_west.wait_recv()
    start_vertical(verticals[2])
    ig_west.start()
    ig_east.start()
    for pair in verticals:
        wait_vertical(pair)

    flat_x = xh[...].reshape(FLAT, CH)
    m_copies = []
    for s in range(GROUPS):
        ks = pl.ds(s * KG, KG)
        m = jnp.dot(op[s * KG : (s + 1) * KG].reshape(KG * CELLS, FLAT), flat_x, preferred_element_type=F32)
        m = m.astype(BF16).reshape(KG, CELLS, CH)
        mfull[s * KG : (s + 1) * KG] = m
        lo, hi = m[:, :, 0:HALF], m[:, :, HALF:CH]
        msend[s * KG : (s + 1) * KG] = jnp.where(core == 0, hi, lo)
        mm[s * KG : (s + 1) * KG, 0:CELLS] = jnp.where(core == 0, lo, hi)
        c = remote(msend.at[ks], mm.at[ks, pl.ds(CELLS, CELLS)], msem_s.at[s], msem_r.at[s], partner)
        c.start()
        m_copies.append(c)

    scale = 1.0 / math.sqrt(CELLS * 512)
    own = pl.ds(pl.multiple_of(rank * SLICE, SLICE), SLICE)
    for s in range(GROUPS):
        m_copies[s].wait_recv()
        for k in range(s * KG, (s + 1) * KG):
            part = jnp.dot(gt[...], mm[k], preferred_element_type=F32) * scale
            dws[k] = part.astype(BF16)
        for d in range(1, 16):
            peer_rows = pl.ds(pl.multiple_of(lax.rem(rank + d, 16) * SLICE, SLICE), SLICE)
            remote(
                dws.at[pl.ds(s * KG, KG), peer_rows], rsb.at[s, d - 1], rs_s.at[s], rs_r.at[s], plane_peer(d)
            ).start()

    acc = jnp.zeros((CELLS, CH), F32)
    for k in range(K):
        acc += lax.dot_general(mfull[k], w_ref[k], (((1,), (1,)), ((), ())), preferred_element_type=F32)
    out_ref[...] = acc.astype(BF16).reshape(ROWS, COLS, CH)

    for s in range(GROUPS):
        whole_wait(rsb.at[s], rs_r.at[s])
        part = dws[s * KG : (s + 1) * KG, own, :].astype(F32)
        for d in range(15):
            part += rsb[s, d].astype(F32)
        zs[s] = part.astype(BF16)

        @pl.when(z4 != s)
        def _():
            slot = lax.rem(z4 - s + 4, 4) - 1
            remote(zs.at[s], zb.at[slot], z_s.at[s], z_r, z4_peer(s)).start()

    @pl.when(z4 < GROUPS)
    def _():
        whole_wait(zb, z_r)
        part = zs[z4].astype(F32)
        for d in range(3):
            part += zb[d].astype(F32)
        zg[zgroup] = part.astype(BF16)
        for d in range(1, 4):
            remote(
                zg.at[zgroup], zg.at[zgroup], zg_s, zg_r, zfar_peer(lax.rem(zgroup + d, 4))
            ).start()

    ig_east.wait_recv()
    ig_west.wait_recv()
    total = mid[:, COLS : 2 * COLS] + lon_in[0].astype(F32) + lon_in[1].astype(F32)
    ig_ref[...] = total.astype(BF16)

    @pl.when(z4 < GROUPS)
    def _():
        whole_wait(zgd, zg_r)
        part = zg[0].astype(F32)
        for d in range(1, 4):
            part += zg[d].astype(F32)
        fin[z4] = part.astype(BF16)
        for d in range(1, 4):
            remote(fin.at[z4], fin.at[z4], fin_s, fin_r.at[z4], z4_peer(lax.rem(z4 + d, 4))).start()

    for s in range(GROUPS):
        @pl.when(z4 != s)
        def _():
            whole_wait(fin.at[s], fin_r.at[s])

        ks = pl.ds(s * KG, KG)
        for d in range(1, 16):
            remote(fin.at[s], dwv.at[ks, own], ag_s.at[s], ag_r.at[s], plane_peer(d)).start()
        dwv[s * KG : (s + 1) * KG, own, :] = fin[s]

    half = pl.ds(pl.multiple_of(core * HALF, HALF), HALF)
    tails = []
    for s in range(GROUPS):
        ks = pl.ds(s * KG, KG)
        whole_wait(rsb.at[s], ag_r.at[s])
        c = remote(dwv.at[ks], dw_ref.at[ks, :, half], fw_s.at[s], fw_r.at[s], partner)
        c.start()
        e = pltpu.make_async_copy(dwv.at[ks], dw_ref.at[ks, :, half], loc.at[s])
        e.start()
        tails.append((c, e))

    for s in range(GROUPS):
        whole_wait(rsb.at[s], rs_s.at[s])
        whole_wait(rsb.at[s], ag_s.at[s])

        @pl.when(z4 != s)
        def _():
            whole_wait(zs.at[s], z_s.at[s])

        m_copies[s].wait_send()

    @pl.when(z4 < GROUPS)
    def _():
        whole_wait(zgd, zg_s)
        whole_wait(zgd, fin_s)

    g_send.wait_send()
    to_east.wait_send()
    to_west.wait_send()
    ig_east.wait_send()
    ig_west.wait_send()

    @pl.when(has_up)
    def _():
        for pair in verticals + ((ig_up, ig_down),):
            pair[0].wait_send()

    @pl.when(has_down)
    def _():
        for pair in verticals + ((ig_up, ig_down),):
            pair[1].wait_send()

    for c, e in tails:
        c.wait()
        e.wait()


def on_device(inputs, out_grad, weight, kernel_basis, band_start, band_width, lon_reach):
    vmem = pl.BlockSpec(memory_space=pltpu.VMEM)
    smem = pl.BlockSpec(memory_space=pltpu.SMEM)
    hbm = pl.BlockSpec(memory_space=pl.ANY)
    dma = pltpu.SemaphoreType.DMA
    scratch = [
        pltpu.VMEM((EXT, PITCH, CH), BF16),
        pltpu.VMEM((ROWS, 32, 128), F32),
        pltpu.VMEM((ROWS, 24, 128), F32),
        pltpu.VMEM((K, CELLS, FLAT), BF16),
        pltpu.VMEM((K, CH, CELLS), BF16),
        pltpu.VMEM((CH, K * CELLS), BF16),
        pltpu.VMEM((ROWS, 3 * COLS, CH), F32),
        pltpu.VMEM((2, ROWS, 3 * COLS, CH), BF16),
        pltpu.VMEM((2, ROWS, 3 * COLS, CH), BF16),
        pltpu.VMEM((2, ROWS, COLS, CH), BF16),
        pltpu.VMEM((2, ROWS, COLS, CH), BF16),
        pltpu.VMEM((CH, 2 * CELLS), BF16),
        pltpu.VMEM((ROWS, COLS, CH), BF16),
        pltpu.VMEM((K, CELLS, CH), BF16),
        pltpu.VMEM((K, 2 * CELLS, HALF), BF16),
        pltpu.VMEM((K, CELLS, HALF), BF16),
        pltpu.VMEM((K, CH, HALF), BF16),
        pltpu.VMEM((GROUPS, 15, KG, SLICE, HALF), BF16),
        pltpu.VMEM((GROUPS, KG, SLICE, HALF), BF16),
        pltpu.VMEM((3, KG, SLICE, HALF), BF16),
        pltpu.VMEM((4, KG, SLICE, HALF), BF16),
        pltpu.VMEM((3, KG, SLICE, HALF), BF16),
        pltpu.VMEM((GROUPS, KG, SLICE, HALF), BF16),
        pltpu.VMEM((K, CH, HALF), BF16),
        dma((8,)), dma((8,)), dma((2,)), dma((4,)), dma((4,)), dma((3,)), dma((3,)),
        dma((3,)), dma((3,)), dma((3,)), dma, dma, dma, dma, dma((3,)), dma((3,)), dma((3,)),
        dma((3,)), dma((3,)), dma((3,)),
    ]
    out, ig, dw = pl.pallas_call(
        kernel,
        out_shape=(
            jax.ShapeDtypeStruct((ROWS, COLS, CH), BF16),
            jax.ShapeDtypeStruct((ROWS, COLS, CH), BF16),
            jax.ShapeDtypeStruct((K, CH, CH), BF16),
        ),
        in_specs=[vmem, vmem, vmem, vmem, smem, smem, smem],
        out_specs=(vmem, vmem, hbm),
        scratch_shapes=scratch,
        compiler_params=pltpu.CompilerParams(collective_id=0, has_side_effects=True, vmem_limit_bytes=40 << 20),
    )(inputs, out_grad, weight, kernel_basis, band_start, band_width, lon_reach)
    return out, ig, dw.astype(F32)


def solution(mesh):
    placed = (
        P("lat", "lon", None),
        P("lat", "lon", None),
        P(),
        P("lat", None, None, None),
        P("lat"),
        P("lat"),
        P("lat"),
    )
    return jax.shard_map(
        on_device,
        mesh=mesh,
        in_specs=placed,
        out_specs=(P("lat", "lon", None), P("lat", "lon", None), P()),
        check_vma=False,
    )
```

time: 699 us -> 81.5 us (0.12)
  waiting for transfers between devices: 476 us -> 0 us
  Pallas kernels: 0 us -> 71.8 us
  starting transfers between devices: 70.1 us -> 0 us
  matrix products: 66.2 us -> 0 us
  loops' own time: 35.7 us -> 0 us
  local copies, waits for them, and re-layouts: 25.8 us -> 7.21 us
  between operations: 14.2 us -> 0.66 us
    psum x1 -> x0, waiting for transfers between devices: 472 us -> none  [on_device(): weight_grad = lax.psum(local_grad, ('lat', 'lon'))]
    pallas_call x0 -> x1, Pallas kernels: none -> 71.8 us  [on_device(): pl.pallas_call(kernel, out_shape=(jax.ShapeDtypeStruct((ROWS, COLS, CH),...]
    ppermute x8 -> x0, starting transfers between devices: 70 us -> none  [the longest x4 39.3 us: extended_2(): lax.ppermute(head, axis, [((i + 1) % count, i) for i in range(ends)])]
    dot_general x39 -> x0, matrix products: 66.2 us -> none  [the longest x18 28.9 us: forward_operator(): jnp.einsum('ibjm,ieb->ijem', spread, row_pick, preferred_element_type=jnp...]
    another operation x2 -> x0, loops' own time: 35.7 us -> none  [the longest x1 17.9 us: on_device(): lax.scan(return_step, jnp.zeros((ext_rows * ext_cols, channels), jnp.floa...]
    dynamic_slice x18 -> x0, local copies, waits for them, and re-layouts: 10.5 us -> none  [on_device(): mixed_in = lax.map(contract, basis_ids)]
    reshape x18 -> x0, local copies, waits for them, and re-layouts: 9.57 us -> none  [forward_operator(): return placed.reshape(rows_here * columns, ext_rows * ext_cols)]
  transfers between devices with their start and end apart: 9 -> 0, of which waited for: 3 -> 0; matrix products, arithmetic and copies ran while one was open for 14% -> 0% of each run, Pallas kernels for 0% -> 0%
where the time goes in v1:
time: 81.5 us; the launch traced here: 81.2 us
  Pallas kernels  71.8 us (88%)
  local copies, waits for them, and re-layouts  7.21 us (9%)
  other arithmetic  1.63 us (2%)
    pallas_call x1, Pallas kernels, on_device(): pl.pallas_call(kernel, out_shape=(jax.ShapeDtypeStruct((ROWS, COLS, CH),...  71.8 us
    unnamed x15, local copies, waits for them, and re-layouts  7.21 us

profile of v1, /device:TPU:1, one launch (start us, length us, event | category | flops | bytes accessed | tf_op | source)
XLA Modules:
  0.0 81.2 jit_solution(11172700986406503793)
XLA Ops:
  0.6 1.0 %copy.10.kb_ref = bf16[8,9,17,33]{3,2,1,0:T(8,128)(2,1)S(1)} copy(bf16[8,9,17,33]{3,0,2,1:T(8,128)(2,1)} %param.10) | data formatting | bytes 161568 | tf_op args[3]
  1.7 0.0 copy-start
  1.7 1.3 %copy-done = bf16[9,256,256]{2,1,0:T(8,128)(2,1)S(1)} copy-done((bf16[9,256,256]{2,1,0:T(8,128)(2,1)S(1)}, bf16[9,256,256]{2,1,0:T(8,128)(2,1)}, u32[]{:S(2)}) %copy-start) | copy-done | bytes 1179672
  2.9 0.0 copy-start.1
  3.0 0.8 %copy-done.1 = bf16[8,16,256]{2,1,0:T(8,128)(2,1)S(1)} copy-done((bf16[8,16,256]{2,1,0:T(8,128)(2,1)S(1)}, bf16[8,16,256]{2,1,0:T(8,128)(2,1)}, u32[]{:S(2)}) %copy-start.1) | copy-done | bytes 65560
  3.8 0.0 copy-start.2
  3.8 0.8 %copy-done.2 = bf16[8,16,256]{2,1,0:T(8,128)(2,1)S(1)} copy-done((bf16[8,16,256]{2,1,0:T(8,128)(2,1)S(1)}, bf16[8,16,256]{2,1,0:T(8,128)(2,1)}, u32[]{:S(2)}) %copy-start.2) | copy-done | bytes 65560
  4.6 0.0 copy-start.3
  4.6 0.7 copy-done.3
  5.3 0.0 copy-start.4
  5.3 0.7 copy-done.4
  5.9 0.0 copy-start.5
  5.9 0.7 copy-done.5
  6.6 71.8 %shard_map.94 = (bf16[8,16,256]{2,1,0:T(8,128)(2,1)S(1)}, bf16[8,16,256]{2,1,0:T(8,128)(2,1)S(1)}, bf16[9,256,256]{2,1,0:T(8,128)(2,1)S(1)}) custom-call(bf16[8,16,256]{2,1,0:T(8,128)(2,1)S(1)} %copy-done.1, bf16[8,16,256]{2,1,0:T(8,128)(2,1)S(1)} %copy-done.2, bf16[9,256,256]{2,1,0:T(8,128)(2,1)S(1)} %copy-done, bf16[8,9,17,33]{3,2,1,0:T(8,128)(2,1)S(1)} %copy.10.kb_ref, ...), custom_call_target="tpu_custom_call" | custom-call | tf_op jit(solution)/shard_map/pallas_call | solution.py:364
  78.4 1.6 %convert_element_type.3 = f32[9,256,256]{2,1,0:T(8,128)} convert(bf16[9,256,256]{2,1,0:T(8,128)(2,1)S(1)} %get-tuple-element.8) | non-fusion elementwise | flops 589824 | bytes 3538944 | tf_op jit(solution)/shard_map/convert_element_type | solution.py:376
  80.0 0.6 copy.13
  80.6 0.6 copy.14
Async XLA Ops:
  1.7 1.3 %copy-start = (bf16[9,256,256]{2,1,0:T(8,128)(2,1)S(1)}, bf16[9,256,256]{2,1,0:T(8,128)(2,1)}, u32[]{:S(2)}) copy-start(bf16[9,256,256]{2,1,0:T(8,128)(2,1)} %w_ref.1) | copy-start | bytes 3538948
  2.9 0.8 %copy-start.1 = (bf16[8,16,256]{2,1,0:T(8,128)(2,1)S(1)}, bf16[8,16,256]{2,1,0:T(8,128)(2,1)}, u32[]{:S(2)}) copy-start(bf16[8,16,256]{2,1,0:T(8,128)(2,1)} %x_ref.1) | copy-start | bytes 196612
  3.8 0.8 %copy-start.2 = (bf16[8,16,256]{2,1,0:T(8,128)(2,1)S(1)}, bf16[8,16,256]{2,1,0:T(8,128)(2,1)}, u32[]{:S(2)}) copy-start(bf16[8,16,256]{2,1,0:T(8,128)(2,1)} %g_ref.1) | copy-start | bytes 196612
  4.6 0.7 copy-start.3
  5.3 0.7 copy-start.4
  5.9 0.7 copy-start.5

commit v2 on v1

v2 whole, which is shorter than its diff:
```python
import functools
import math

import jax
import jax.numpy as jnp
from jax import lax
from jax.experimental import pallas as pl
from jax.experimental.pallas import tpu as pltpu
from jax.sharding import PartitionSpec as P

MESH = pl.DeviceIdType.MESH
F32, BF16 = jnp.float32, jnp.bfloat16

ROWS, COLS, CH = 8, 16, 256
CELLS = ROWS * COLS
K, BAND, LONW = 9, 17, 33
EXT = 3 * ROWS
PITCH = 64
FLAT = EXT * PITCH
PAIRS = EXT // 2
HALF = 128
GROUPS = 3
KG = K // GROUPS
SLICE = 16


def whole_wait(buf, sem):
    pltpu.make_async_copy(buf, buf, sem).wait()


def kernel(
    x_ref, g_ref, w_ref, kb_ref, start_ref, width_ref, reach_ref,
    out_ref, ig_ref, dw_ref,
    start_v, width_v, reach_v, wv, kbv, mask, kbs, comb, op,
    xh, xtc, xc, em, xt, gs, mt, mg, mgt, mid, lat_out, lat_in, lon_out, lon_in, mfull,
    wcs, wcr, zs, zb, zg, zgd, fin, dwv, dwt, eye,
    lsem, xsend, xrecv, xa_s, xa_r, seam_s, seam_r, fsend, frecv, g_s, g_r, igsend, igrecv, wsem,
    z_s, z_r, zg_s, zg_r, fin_s, fin_r, ag_s, ag_r, fw_s, fw_r, loc,
):
    lat, lon = lax.axis_index("lat"), lax.axis_index("lon")
    core = lax.rem(lat, 2)
    zlo = lat // 2
    zhi = lon // 16
    rank = lax.rem(lon, 16)
    z4 = lax.rem(zlo, 4)
    zgroup = zhi * 2 + zlo // 4
    up, down = lat - 1, lat + 1
    has_up, has_down = lat > 0, lat < 15
    east, west = lax.rem(lon + 1, 32), lax.rem(lon + 31, 32)
    partner = (lat + 1 - 2 * core, lon)
    first_sector, last_sector = rank == 0, rank == 15

    def plane_peer(d):
        return (lat, zhi * 16 + lax.rem(rank + d, 16))

    def other_half(t):
        return (lat, (1 - zhi) * 16 + t)

    def z4_peer(t):
        return ((zlo - z4 + t) * 2 + core, lon)

    def zfar_peer(t):
        return (((t % 2) * 4 + z4) * 2 + core, (t // 2) * 16 + rank)

    def remote(src, dst, ssem, rsem, dev):
        return pltpu.make_async_remote_copy(
            src_ref=src, dst_ref=dst, send_sem=ssem, recv_sem=rsem, device_id=dev, device_id_type=MESH
        )

    mid_rows, top, bottom = pl.ds(ROWS, ROWS), pl.ds(0, ROWS), pl.ds(2 * ROWS, ROWS)
    mid_cols, wcols, ecols = pl.ds(COLS, COLS), pl.ds(0, COLS), pl.ds(2 * COLS, COLS)

    local = [
        pltpu.make_async_copy(kb_ref, kbv, lsem.at[0]),
        pltpu.make_async_copy(start_ref, start_v, lsem.at[1]),
        pltpu.make_async_copy(width_ref, width_v, lsem.at[2]),
        pltpu.make_async_copy(reach_ref, reach_v, lsem.at[3]),
        pltpu.make_async_copy(g_ref, gs.at[rank], lsem.at[4]),
        pltpu.make_async_copy(w_ref, wv, lsem.at[5]),
        pltpu.make_async_copy(x_ref, xh.at[mid_rows, mid_cols], lsem.at[6]),
    ]
    for c in local[:-1]:
        c.start()
    xh[...] = jnp.zeros_like(xh)
    local[-1].start()
    xc[...] = jnp.zeros_like(xc)
    lat_in[...] = jnp.zeros_like(lat_in)

    bar = pltpu.get_barrier_semaphore()

    def signal(dev):
        pl.semaphore_signal(bar, inc=1, device_id=dev, device_id_type=MESH)

    signal(other_half(0))
    signal(other_half(15))
    signal((lat, east))
    signal((lat, west))
    for d in range(1, 4):
        signal(zfar_peer(lax.rem(zgroup + d, 4)))
    for d in range(1, 16):
        signal(plane_peer(d))
    for d in range(1, 4):
        signal(z4_peer(lax.rem(z4 + d, 4)))

    @pl.when(has_up)
    def _():
        signal((up, lon))

    @pl.when(has_down)
    def _():
        signal((down, lon))

    kbs[...] = jnp.zeros_like(kbs)
    row = lax.broadcasted_iota(jnp.int32, (ROWS, ROWS), 0)
    eye[...] = (
        lax.broadcasted_iota(jnp.int32, (CH, CH), 0) == lax.broadcasted_iota(jnp.int32, (CH, CH), 1)
    ).astype(F32).astype(BF16)
    cell = lax.broadcasted_iota(jnp.int32, (3 * CELLS, ROWS * PITCH), 0)
    place = (cell % CELLS) // COLS * PITCH + cell // CELLS * COLS + cell % COLS
    em[...] = (place == lax.broadcasted_iota(jnp.int32, (3 * CELLS, ROWS * PITCH), 1)).astype(F32).astype(BF16)

    for c in local[:4]:
        c.wait()
    row = lax.broadcasted_iota(jnp.int32, (BAND, ROWS, LONW), 1)
    band_pos = lax.broadcasted_iota(jnp.int32, (BAND, ROWS, LONW), 0)
    lon_off = jnp.abs(lax.broadcasted_iota(jnp.int32, (BAND, ROWS, LONW), 2) - (LONW - 1) // 2)
    inside = jnp.zeros((BAND, ROWS, LONW), jnp.bool_)
    for i in range(ROWS):
        first = start_v[i]
        keep = (band_pos >= first) & (band_pos < first + width_v[i]) & (lon_off <= reach_v[i])
        inside = inside | (keep & (row == i))
    mask[...] = inside.astype(F32)

    def op_step(k, carry):
        kbs[1 : 1 + BAND, :, 0:LONW] = jnp.where(mask[...] > 0.5, kbv[k].astype(F32), 0.0)
        for t in range(BAND + 1):
            comb[t] = kbs[t] + pltpu.roll(kbs[t + 1], PITCH, 1)
        for i in range(ROWS):
            for q in range(PAIRS):
                t = 2 * q - i + 1
                if 0 <= t <= BAND:
                    line = jnp.broadcast_to(comb[t, i : i + 1, :], (COLS, 128))
                    tile = pltpu.roll(line, 0, 1, stride=1, stride_axis=0)
                    op[k, i * COLS : (i + 1) * COLS, q * 128 : (q + 1) * 128] = tile.astype(BF16)
                else:
                    op[k, i * COLS : (i + 1) * COLS, q * 128 : (q + 1) * 128] = jnp.zeros((COLS, 128), BF16)
        return carry

    lax.fori_loop(0, K, op_step, 0)

    local[6].wait()
    xtc[...] = xh[mid_rows, mid_cols, :].reshape(CELLS, CH).astype(F32).T.astype(BF16)
    own = pl.ds(pl.multiple_of(rank * SLICE, SLICE), SLICE)
    xc[1, 1 + rank] = xtc[own, :]

    at_seam = jnp.logical_or(first_sector, last_sector).astype(jnp.int32)
    pl.semaphore_wait(bar, 23 + has_up.astype(jnp.int32) + has_down.astype(jnp.int32) + 16 * at_seam)

    @pl.when(last_sector)
    def _():
        for t in range(16):
            remote(xtc.at[pl.ds(t * SLICE, SLICE)], xc.at[1, 0], seam_s.at[0], seam_r.at[0], other_half(t)).start()

    @pl.when(first_sector)
    def _():
        for t in range(16):
            remote(xtc.at[pl.ds(t * SLICE, SLICE)], xc.at[1, 17], seam_s.at[1], seam_r.at[1], other_half(t)).start()

    for d in range(1, 16):
        peer_rows = pl.ds(pl.multiple_of(lax.rem(rank + d, 16) * SLICE, SLICE), SLICE)
        remote(xtc.at[peer_rows], xc.at[1, 1 + rank], xa_s, xa_r, plane_peer(d)).start()
    local[4].wait()
    for d in range(1, 16):
        remote(gs.at[rank], gs.at[rank], g_s, g_r, plane_peer(d)).start()

    local[5].wait()
    g = gs[rank]

    for k in range(K):
        part = jnp.dot(g, wv[k], preferred_element_type=F32).astype(BF16)
        part = lax.dot_general(eye[...], part, (((1,), (1,)), ((), ())), preferred_element_type=F32)
        mgt[:, k * CELLS : (k + 1) * CELLS] = part.astype(BF16)

    for n in range(FLAT // 256):
        part = jnp.dot(
            mgt[...], op[:, :, n * 256 : (n + 1) * 256].reshape(K * CELLS, 256), preferred_element_type=F32
        )
        part = part.T.reshape(4, PITCH, CH)[:, : 3 * COLS]
        r = n * 4
        if r < ROWS:
            lat_out[0, r : r + 4] = part.astype(BF16)
        elif r < 2 * ROWS:
            mid[r - ROWS : r - ROWS + 4] = part
        else:
            lat_out[1, r - 2 * ROWS : r - 2 * ROWS + 4] = part.astype(BF16)

    def start_vertical(pair):
        @pl.when(has_up)
        def _():
            pair[0].start()

        @pl.when(has_down)
        def _():
            pair[1].start()

    def wait_vertical(pair):
        @pl.when(has_down)
        def _():
            pair[0].wait_recv()

        @pl.when(has_up)
        def _():
            pair[1].wait_recv()

    def forward(slots, s):
        src = xc.at[1, slots]
        return (
            remote(src, xc.at[2, slots], fsend.at[s], frecv.at[s], (up, lon)),
            remote(src, xc.at[0, slots], fsend.at[s + 1], frecv.at[s + 1], (down, lon)),
        )

    forwards = (forward(pl.ds(1, 16), 0), forward(pl.ds(0, 1), 2), forward(pl.ds(17, 1), 4))
    whole_wait(xc.at[1, pl.ds(1, 15)], xa_r)
    start_vertical(forwards[0])
    ig_up = remote(lat_out.at[0], lat_in.at[1], igsend.at[0], igrecv.at[0], (up, lon))
    ig_down = remote(lat_out.at[1], lat_in.at[0], igsend.at[1], igrecv.at[1], (down, lon))
    start_vertical((ig_up, ig_down))

    to_east = remote(x_ref, xh.at[mid_rows, wcols], xsend.at[0], xrecv.at[0], (lat, east))
    to_west = remote(x_ref, xh.at[mid_rows, ecols], xsend.at[1], xrecv.at[1], (lat, west))
    to_east.start()
    to_west.start()

    def up_down(cols, s):
        src = xh.at[mid_rows, cols]
        return (
            remote(src, xh.at[bottom, cols], xsend.at[s], xrecv.at[s], (up, lon)),
            remote(src, xh.at[top, cols], xsend.at[s + 1], xrecv.at[s + 1], (down, lon)),
        )

    verticals = (up_down(mid_cols, 2), up_down(wcols, 4), up_down(ecols, 6))
    start_vertical(verticals[0])

    for s in range(2):
        whole_wait(xc.at[1, 0], seam_r.at[s])
        start_vertical(forwards[1 + s])

    for pair in forwards:
        wait_vertical(pair)
    whole_wait(gs.at[pl.ds(0, 15)], g_r)

    for b in range(3):
        part = jnp.zeros((CH, ROWS * PITCH), F32)
        for d in range(3):
            part += jnp.dot(
                xc[b, d : d + 16].reshape(CH, CELLS), em[d * CELLS : (d + 1) * CELLS], preferred_element_type=F32
            )
        xt[:, b * ROWS * PITCH : (b + 1) * ROWS * PITCH] = part.astype(BF16)
    for s in range(GROUPS):
        part = lax.dot_general(
            xt[...], op[s * KG : (s + 1) * KG].reshape(KG * CELLS, FLAT), (((1,), (1,)), ((), ())),
            preferred_element_type=F32,
        ).astype(BF16)
        for k in range(KG):
            for t in range(16):
                mt[s * KG + k, :, t * CELLS : (t + 1) * CELLS] = part[
                    t * SLICE : (t + 1) * SLICE, k * CELLS : (k + 1) * CELLS
                ]
    scale = 1.0 / math.sqrt(CELLS * 512)
    dwp = jnp.dot(
        mt[...].reshape(K * SLICE, 16 * CELLS), gs[...].reshape(16 * CELLS, CH), preferred_element_type=F32
    )
    dwp = (dwp * scale).reshape(K, SLICE, CH)

    wcs[...] = jnp.where(core == 0, dwp[:, :, HALF:CH], dwp[:, :, 0:HALF])
    w_copy = remote(wcs, wcr, wsem.at[0], wsem.at[1], partner)
    w_copy.start()
    keep_half = jnp.where(core == 0, dwp[:, :, 0:HALF], dwp[:, :, HALF:CH])
    w_copy.wait_recv()
    keep_half = keep_half + wcr[...]

    for s in range(GROUPS):
        zs[s] = keep_half[s * KG : (s + 1) * KG].astype(BF16)

        @pl.when(z4 != s)
        def _():
            slot = lax.rem(z4 - s + 4, 4) - 1
            remote(zs.at[s], zb.at[slot], z_s.at[s], z_r, z4_peer(s)).start()

    wait_vertical((ig_up, ig_down))
    total = mid[...] + lat_in[0].astype(F32) + lat_in[1].astype(F32)
    lon_out[0] = total[:, 0:COLS].astype(BF16)
    lon_out[1] = total[:, 2 * COLS : 3 * COLS].astype(BF16)
    mid[:, COLS : 2 * COLS] = total[:, COLS : 2 * COLS]
    ig_west = remote(lon_out.at[0], lon_in.at[1], igsend.at[2], igrecv.at[2], (lat, west))
    ig_east = remote(lon_out.at[1], lon_in.at[0], igsend.at[3], igrecv.at[3], (lat, east))
    ig_west.start()
    ig_east.start()

    @pl.when(z4 < GROUPS)
    def _():
        whole_wait(zb, z_r)
        part = zs[z4].astype(F32)
        for d in range(3):
            part += zb[d].astype(F32)
        zg[zgroup] = part.astype(BF16)
        for d in range(1, 4):
            remote(
                zg.at[zgroup], zg.at[zgroup], zg_s, zg_r, zfar_peer(lax.rem(zgroup + d, 4))
            ).start()

    to_east.wait_recv()
    start_vertical(verticals[1])
    to_west.wait_recv()
    start_vertical(verticals[2])
    for pair in verticals:
        wait_vertical(pair)

    flat_x = xh[...].reshape(FLAT, CH)
    acc = jnp.zeros((CELLS, CH), F32)
    for s in range(GROUPS):
        m = jnp.dot(op[s * KG : (s + 1) * KG].reshape(KG * CELLS, FLAT), flat_x, preferred_element_type=F32)
        m = m.astype(BF16).reshape(KG, CELLS, CH)
        for k in range(KG):
            acc += lax.dot_general(m[k], wv[s * KG + k], (((1,), (1,)), ((), ())), preferred_element_type=F32)
    out_ref[...] = acc.astype(BF16).reshape(ROWS, COLS, CH)

    @pl.when(z4 < GROUPS)
    def _():
        whole_wait(zgd, zg_r)
        part = zg[0].astype(F32)
        for d in range(1, 4):
            part += zg[d].astype(F32)
        fin[z4] = part.astype(BF16)
        for d in range(1, 4):
            remote(fin.at[z4], fin.at[z4], fin_s, fin_r.at[z4], z4_peer(lax.rem(z4 + d, 4))).start()

    for s in range(GROUPS):
        @pl.when(z4 != s)
        def _():
            whole_wait(fin.at[s], fin_r.at[s])

        ks = pl.ds(s * KG, KG)
        for d in range(1, 16):
            remote(fin.at[s], dwv.at[ks, own], ag_s.at[s], ag_r.at[s], plane_peer(d)).start()
        dwv[s * KG : (s + 1) * KG, own, :] = fin[s]

    ig_east.wait_recv()
    ig_west.wait_recv()
    total = mid[:, COLS : 2 * COLS] + lon_in[0].astype(F32) + lon_in[1].astype(F32)
    ig_ref[...] = total.astype(BF16)

    half = pl.ds(pl.multiple_of(core * HALF, HALF), HALF)
    small_eye = eye[0:HALF, 0:HALF]
    tails = []
    for s in range(GROUPS):
        ks = pl.ds(s * KG, KG)
        whole_wait(dwv.at[ks, pl.ds(0, 15 * SLICE)], ag_r.at[s])
        for k in range(s * KG, (s + 1) * KG):
            part = lax.dot_general(small_eye, dwv[k], (((1,), (1,)), ((), ())), preferred_element_type=F32)
            dwt[k] = part.astype(BF16)
        c = remote(dwt.at[ks], dw_ref.at[ks, half], fw_s.at[s], fw_r.at[s], partner)
        c.start()
        e = pltpu.make_async_copy(dwt.at[ks], dw_ref.at[ks, half], loc.at[s])
        e.start()
        tails.append((c, e))

    for s in range(GROUPS):
        whole_wait(dwv.at[pl.ds(s * KG, KG), pl.ds(0, 15 * SLICE)], ag_s.at[s])

        @pl.when(z4 != s)
        def _():
            whole_wait(zs.at[s], z_s.at[s])

    @pl.when(z4 < GROUPS)
    def _():
        whole_wait(zgd, zg_s)
        whole_wait(zgd, fin_s)

    @pl.when(last_sector)
    def _():
        whole_wait(xtc, seam_s.at[0])

    @pl.when(first_sector)
    def _():
        whole_wait(xtc, seam_s.at[1])

    whole_wait(xc.at[1, pl.ds(1, 15)], xa_s)
    whole_wait(gs.at[pl.ds(0, 15)], g_s)
    w_copy.wait_send()
    to_east.wait_send()
    to_west.wait_send()
    ig_east.wait_send()
    ig_west.wait_send()

    @pl.when(has_up)
    def _():
        for pair in verticals + forwards + ((ig_up, ig_down),):
            pair[0].wait_send()

    @pl.when(has_down)
    def _():
        for pair in verticals + forwards + ((ig_up, ig_down),):
            pair[1].wait_send()

    for c, e in tails:
        c.wait()
        e.wait()


def on_device(inputs, out_grad, weight, kernel_basis, band_start, band_width, lon_reach):
    vmem = pl.BlockSpec(memory_space=pltpu.VMEM)
    hbm = pl.BlockSpec(memory_space=pl.ANY)
    dma = pltpu.SemaphoreType.DMA
    piece = (KG, SLICE, HALF)
    scratch = [
        pltpu.SMEM((ROWS,), jnp.int32),
        pltpu.SMEM((ROWS,), jnp.int32),
        pltpu.SMEM((ROWS,), jnp.int32),
        pltpu.VMEM((K, CH, CH), BF16),
        pltpu.VMEM((K, BAND, ROWS, LONW), BF16),
        pltpu.VMEM((BAND, ROWS, LONW), F32),
        pltpu.VMEM((BAND + 2, ROWS, 128), F32),
        pltpu.VMEM((BAND + 1, ROWS, 128), F32),
        pltpu.VMEM((K, CELLS, FLAT), BF16),
        pltpu.VMEM((EXT, PITCH, CH), BF16),
        pltpu.VMEM((CH, CELLS), BF16),
        pltpu.VMEM((3, 18, SLICE, CELLS), BF16),
        pltpu.VMEM((3 * CELLS, ROWS * PITCH), BF16),
        pltpu.VMEM((CH, FLAT), BF16),
        pltpu.VMEM((16, CELLS, CH), BF16),
        pltpu.VMEM((K, SLICE, 16 * CELLS), BF16),
        pltpu.VMEM((K, CH, CELLS), BF16),
        pltpu.VMEM((CH, K * CELLS), BF16),
        pltpu.VMEM((ROWS, 3 * COLS, CH), F32),
        pltpu.VMEM((2, ROWS, 3 * COLS, CH), BF16),
        pltpu.VMEM((2, ROWS, 3 * COLS, CH), BF16),
        pltpu.VMEM((2, ROWS, COLS, CH), BF16),
        pltpu.VMEM((2, ROWS, COLS, CH), BF16),
        pltpu.VMEM((K, CELLS, CH), BF16),
        pltpu.VMEM((K, SLICE, HALF), F32),
        pltpu.VMEM((K, SLICE, HALF), F32),
        pltpu.VMEM((GROUPS,) + piece, BF16),
        pltpu.VMEM((3,) + piece, BF16),
        pltpu.VMEM((4,) + piece, BF16),
        pltpu.VMEM((3,) + piece, BF16),
        pltpu.VMEM((GROUPS,) + piece, BF16),
        pltpu.VMEM((K, CH, HALF), BF16),
        pltpu.VMEM((K, HALF, CH), BF16),
        pltpu.VMEM((CH, CH), BF16),
        dma((7,)), dma((8,)), dma((8,)), dma, dma, dma((2,)), dma((2,)), dma((6,)), dma((6,)), dma, dma,
        dma((4,)), dma((4,)), dma((2,)),
        dma((3,)), dma, dma, dma, dma, dma((3,)), dma((3,)), dma((3,)), dma((3,)), dma((3,)), dma((3,)),
    ]
    out, ig, dw = pl.pallas_call(
        kernel,
        out_shape=(
            jax.ShapeDtypeStruct((ROWS, COLS, CH), BF16),
            jax.ShapeDtypeStruct((ROWS, COLS, CH), BF16),
            jax.ShapeDtypeStruct((K, CH, CH), BF16),
        ),
        in_specs=[hbm] * 7,
        out_specs=(vmem, vmem, hbm),
        scratch_shapes=scratch,
        compiler_params=pltpu.CompilerParams(collective_id=0, has_side_effects=True, vmem_limit_bytes=56 << 20),
    )(
        inputs, out_grad.reshape(CELLS, CH), weight, kernel_basis.transpose(1, 2, 0, 3),
        band_start, band_width, lon_reach,
    )
    return out, ig, dw.astype(F32)


def solution(mesh):
    placed = (
        P("lat", "lon", None),
        P("lat", "lon", None),
        P(),
        P("lat", None, None, None),
        P("lat"),
        P("lat"),
        P("lat"),
    )
    return jax.shard_map(
        on_device,
        mesh=mesh,
        in_specs=placed,
        out_specs=(P("lat", "lon", None), P("lat", "lon", None), P()),
        check_vma=False,
    )
```

time: 81.5 us -> 70.4 us (0.86)
  the two profiles are of different devices: /device:TPU:1 before, /device:TPU:35 now
where the time goes in v2:
time: 70.4 us; the launch traced here: 70.3 us
  Pallas kernels  65.4 us (93%)
  other arithmetic  2.93 us (4%)
  local copies, waits for them, and re-layouts  1.27 us (2%)
    pallas_call x1, Pallas kernels, on_device(): pl.pallas_call(kernel, out_shape=(jax.ShapeDtypeStruct((ROWS, COLS, CH),...  65.4 us
    convert_element_type x1, other arithmetic, on_device(): return (out, ig, dw.astype(F32))  2.93 us

profile of v2, /device:TPU:35, one launch (start us, length us, event | category | flops | bytes accessed | tf_op | source)
XLA Modules:
  0.0 70.3 jit_solution(7423704771803941796)
XLA Ops:
  0.6 65.4 %shard_map.94 = (bf16[8,16,256]{2,1,0:T(8,128)(2,1)}, bf16[8,16,256]{2,1,0:T(8,128)(2,1)}, bf16[9,256,256]{2,1,0:T(8,128)(2,1)}) custom-call(bf16[8,16,256]{2,1,0:T(8,128)(2,1)} %x_ref.1, bf16[128,256]{1,0:T(8,128)(2,1)} %bitcast.3, bf16[9,256,256]{2,1,0:T(8,128)(2,1)} %w_ref.1, bf16[9,17,8,33]{3,2,1,0:T(8,128)(2,1)} %bitcast.2, s32[8]{0:T(128)} %start_ref.1, ...), custom_call_target="tpu_custom_call" | custom-call | tf_op jit(solution)/shard_map/pallas_call | solution.py:455
  66.1 0.0 copy-start.1
  66.1 0.0 copy-start
  66.1 2.9 %convert_element_type.3 = f32[9,256,256]{2,1,0:T(8,128)} convert(bf16[9,256,256]{2,1,0:T(8,128)(2,1)} %get-tuple-element.8) | non-fusion elementwise | flops 589824 | bytes 3538944 | tf_op jit(solution)/shard_map/convert_element_type | solution.py:470
  69.0 0.0 copy-done.1
  69.0 0.6 copy.12
  69.6 0.0 copy-done
  69.6 0.6 copy.13
Async XLA Ops:
  66.1 3.0 %copy-start.1 = (bf16[8,16,256]{2,1,0:T(8,128)(2,1)S(1)}, bf16[8,16,256]{2,1,0:T(8,128)(2,1)}, u32[]{:S(2)}) copy-start(bf16[8,16,256]{2,1,0:T(8,128)(2,1)} %get-tuple-element.12) | copy-start | bytes 196612
  66.1 3.6 %copy-start = (bf16[8,16,256]{2,1,0:T(8,128)(2,1)S(1)}, bf16[8,16,256]{2,1,0:T(8,128)(2,1)}, u32[]{:S(2)}) copy-start(bf16[8,16,256]{2,1,0:T(8,128)(2,1)} %get-tuple-element.13) | copy-start | bytes 196612

commit v3 on v2

v3 whole, which is shorter than its diff:
```python
import functools
import math

import jax
import jax.numpy as jnp
from jax import lax
from jax.experimental import pallas as pl
from jax.experimental.pallas import tpu as pltpu
from jax.sharding import PartitionSpec as P

MESH = pl.DeviceIdType.MESH
F32, BF16 = jnp.float32, jnp.bfloat16

ROWS, COLS, CH = 8, 16, 256
CELLS = ROWS * COLS
K, BAND, LONW = 9, 17, 33
EXT = 3 * ROWS
PITCH = 64
FLAT = EXT * PITCH
PAIRS = EXT // 2
HALF = 128
GROUPS = 3
KG = K // GROUPS
SLICE = 16


def whole_wait(buf, sem):
    pltpu.make_async_copy(buf, buf, sem).wait()


def kernel(
    x_ref, g_ref, w_ref, kb_ref, start_ref, width_ref, reach_ref,
    out_ref, ig_ref, dw_ref,
    start_v, width_v, reach_v, wv, kbv, mask, kbs, comb, op,
    xh, xtc, xc, em, xt, gs, mt, mgt, mid, lat_out, lat_in, lon_out, lon_in, dwp,
    wcs, wcr, zs, zb, zg, zgd, fin, dwv, sg, eye,
    lsem, xsend, xrecv, xa_s, xa_r, seam_s, seam_r, fsend, frecv, g_s, g_r, igsend, igrecv, wsem,
    z_s, z_r, zg_s, zg_r, fin_s, fin_r, ag_s, ag_r, fw_s, fw_r, sg_s, sg_r,
):
    lat, lon = lax.axis_index("lat"), lax.axis_index("lon")
    core = lax.rem(lat, 2)
    zlo = lat // 2
    zhi = lon // 16
    rank = lax.rem(lon, 16)
    z4 = lax.rem(zlo, 4)
    zgroup = zhi * 2 + zlo // 4
    up, down = lat - 1, lat + 1
    has_up, has_down = lat > 0, lat < 15
    east, west = lax.rem(lon + 1, 32), lax.rem(lon + 31, 32)
    partner = (lat + 1 - 2 * core, lon)
    not_first, not_last = rank > 0, rank < 15

    def plane_peer(d):
        return (lat, zhi * 16 + lax.rem(rank + d, 16))

    other_half = (lat, (1 - zhi) * 16 + rank)

    def z4_peer(t):
        return ((zlo - z4 + t) * 2 + core, lon)

    def zfar_peer(t):
        return (((t % 2) * 4 + z4) * 2 + core, (t // 2) * 16 + rank)

    def remote(src, dst, ssem, rsem, dev):
        return pltpu.make_async_remote_copy(
            src_ref=src, dst_ref=dst, send_sem=ssem, recv_sem=rsem, device_id=dev, device_id_type=MESH
        )

    mid_rows, top, bottom = pl.ds(ROWS, ROWS), pl.ds(0, ROWS), pl.ds(2 * ROWS, ROWS)
    mid_cols, wcols, ecols = pl.ds(COLS, COLS), pl.ds(0, COLS), pl.ds(2 * COLS, COLS)

    local = [
        pltpu.make_async_copy(kb_ref, kbv, lsem.at[0]),
        pltpu.make_async_copy(start_ref, start_v, lsem.at[1]),
        pltpu.make_async_copy(width_ref, width_v, lsem.at[2]),
        pltpu.make_async_copy(reach_ref, reach_v, lsem.at[3]),
        pltpu.make_async_copy(g_ref, gs.at[rank], lsem.at[4]),
        pltpu.make_async_copy(w_ref, wv, lsem.at[5]),
        pltpu.make_async_copy(x_ref, xh.at[mid_rows, mid_cols], lsem.at[6]),
    ]
    for c in (local[6],) + tuple(local[:6]):
        c.start()

    @pl.when(jnp.logical_not(has_up))
    def _():
        xh[0:ROWS] = jnp.zeros((ROWS, PITCH, CH), BF16)
        xc[0] = jnp.zeros((18, SLICE, CELLS), BF16)
        lat_in[0] = jnp.zeros((ROWS, 3 * COLS, CH), BF16)

    @pl.when(jnp.logical_not(has_down))
    def _():
        xh[2 * ROWS : EXT] = jnp.zeros((ROWS, PITCH, CH), BF16)
        xc[2] = jnp.zeros((18, SLICE, CELLS), BF16)
        lat_in[1] = jnp.zeros((ROWS, 3 * COLS, CH), BF16)

    bar = pltpu.get_barrier_semaphore()

    def signal(dev):
        pl.semaphore_signal(bar, inc=1, device_id=dev, device_id_type=MESH)

    for d in range(1, 4):
        signal(zfar_peer(lax.rem(zgroup + d, 4)))
    for d in range(1, 16):
        signal(plane_peer(d))
    for d in range(1, 4):
        signal(z4_peer(lax.rem(z4 + d, 4)))

    @pl.when(has_up)
    def _():
        signal((up, lon))

    @pl.when(has_down)
    def _():
        signal((down, lon))

    local[6].wait()
    xtc[...] = xh[mid_rows, mid_cols, :].reshape(CELLS, CH).astype(F32).T.astype(BF16)
    own = pl.ds(pl.multiple_of(rank * SLICE, SLICE), SLICE)
    xc[1, 1 + rank] = xtc[own, :]

    kbs[...] = jnp.zeros_like(kbs)
    xh[:, 3 * COLS : PITCH] = jnp.zeros((EXT, PITCH - 3 * COLS, CH), BF16)
    eye[...] = (
        lax.broadcasted_iota(jnp.int32, (CH, CH), 0) == lax.broadcasted_iota(jnp.int32, (CH, CH), 1)
    ).astype(F32).astype(BF16)
    cell = lax.broadcasted_iota(jnp.int32, (3 * CELLS, ROWS * PITCH), 0)
    place = (cell % CELLS) // COLS * PITCH + cell // CELLS * COLS + cell % COLS
    em[...] = (place == lax.broadcasted_iota(jnp.int32, (3 * CELLS, ROWS * PITCH), 1)).astype(F32).astype(BF16)

    for c in local[:4]:
        c.wait()
    row = lax.broadcasted_iota(jnp.int32, (BAND, ROWS, LONW), 1)
    band_pos = lax.broadcasted_iota(jnp.int32, (BAND, ROWS, LONW), 0)
    lon_off = jnp.abs(lax.broadcasted_iota(jnp.int32, (BAND, ROWS, LONW), 2) - (LONW - 1) // 2)
    inside = jnp.zeros((BAND, ROWS, LONW), jnp.bool_)
    for i in range(ROWS):
        first = start_v[i]
        keep = (band_pos >= first) & (band_pos < first + width_v[i]) & (lon_off <= reach_v[i])
        inside = inside | (keep & (row == i))
    mask[...] = inside.astype(F32)

    def op_step(k, carry):
        kbs[1 : 1 + BAND, :, 0:LONW] = jnp.where(mask[...] > 0.5, kbv[k].astype(F32), 0.0)
        for t in range(BAND + 1):
            comb[t] = kbs[t] + pltpu.roll(kbs[t + 1], PITCH, 1)
        for i in range(ROWS):
            for q in range(PAIRS):
                t = 2 * q - i + 1
                if 0 <= t <= BAND:
                    line = jnp.broadcast_to(comb[t, i : i + 1, :], (COLS, 128))
                    tile = pltpu.roll(line, 0, 1, stride=1, stride_axis=0)
                    op[k, i * COLS : (i + 1) * COLS, q * 128 : (q + 1) * 128] = tile.astype(BF16)
                else:
                    op[k, i * COLS : (i + 1) * COLS, q * 128 : (q + 1) * 128] = jnp.zeros((COLS, 128), BF16)
        return carry

    lax.fori_loop(0, K, op_step, 0)

    pl.semaphore_wait(bar, 21 + has_up.astype(jnp.int32) + has_down.astype(jnp.int32))

    for d in range(1, 16):
        peer_rows = pl.ds(pl.multiple_of(lax.rem(rank + d, 16) * SLICE, SLICE), SLICE)
        remote(xtc.at[peer_rows], xc.at[1, 1 + rank], xa_s, xa_r, plane_peer(d)).start()
    local[4].wait()
    for d in range(1, 16):
        remote(gs.at[rank], gs.at[rank], g_s, g_r, plane_peer(d)).start()


    def start_vertical(pair):
        @pl.when(has_up)
        def _():
            pair[0].start()

        @pl.when(has_down)
        def _():
            pair[1].start()

    def wait_vertical(pair):
        @pl.when(has_down)
        def _():
            pair[0].wait_recv()

        @pl.when(has_up)
        def _():
            pair[1].wait_recv()

    def forward(slots, s):
        src = xc.at[1, slots]
        return (
            remote(src, xc.at[2, slots], fsend.at[s], frecv.at[s], (up, lon)),
            remote(src, xc.at[0, slots], fsend.at[s + 1], frecv.at[s + 1], (down, lon)),
        )

    forwards = (forward(pl.ds(1, 16), 0), forward(pl.ds(0, 1), 2), forward(pl.ds(17, 1), 4))
    whole_wait(xc.at[1, pl.ds(1, 15)], xa_r)
    seams = (
        remote(xc.at[1, 16], xc.at[1, 0], seam_s.at[0], seam_r.at[0], other_half),
        remote(xc.at[1, 1], xc.at[1, 17], seam_s.at[1], seam_r.at[1], other_half),
    )
    for c in seams:
        c.start()
    start_vertical(forwards[0])

    to_east = remote(x_ref, xh.at[mid_rows, wcols], xsend.at[0], xrecv.at[0], (lat, east))
    to_west = remote(x_ref, xh.at[mid_rows, ecols], xsend.at[1], xrecv.at[1], (lat, west))

    @pl.when(not_last)
    def _():
        to_east.start()

    @pl.when(not_first)
    def _():
        to_west.start()

    local[5].wait()
    g = gs[rank]

    for k in range(K):
        part = jnp.dot(g, wv[k], preferred_element_type=F32).astype(BF16)
        part = lax.dot_general(eye[...], part, (((1,), (1,)), ((), ())), preferred_element_type=F32)
        mgt[:, k * CELLS : (k + 1) * CELLS] = part.astype(BF16)

    for n in range(FLAT // 256):
        part = jnp.dot(
            mgt[...], op[:, :, n * 256 : (n + 1) * 256].reshape(K * CELLS, 256), preferred_element_type=F32
        )
        part = part.T.reshape(4, PITCH, CH)[:, : 3 * COLS]
        r = n * 4
        if r < ROWS:
            lat_out[0, r : r + 4] = part.astype(BF16)
        elif r < 2 * ROWS:
            mid[r - ROWS : r - ROWS + 4] = part
        else:
            lat_out[1, r - 2 * ROWS : r - 2 * ROWS + 4] = part.astype(BF16)

    ig_up = remote(lat_out.at[0], lat_in.at[1], igsend.at[0], igrecv.at[0], (up, lon))
    ig_down = remote(lat_out.at[1], lat_in.at[0], igsend.at[1], igrecv.at[1], (down, lon))
    start_vertical((ig_up, ig_down))

    def up_down(cols, s):
        src = xh.at[mid_rows, cols]
        return (
            remote(src, xh.at[bottom, cols], xsend.at[s], xrecv.at[s], (up, lon)),
            remote(src, xh.at[top, cols], xsend.at[s + 1], xrecv.at[s + 1], (down, lon)),
        )

    verticals = (up_down(mid_cols, 2), up_down(wcols, 4), up_down(ecols, 6))
    start_vertical(verticals[0])

    def windows(slots):
        blocks = []
        for b in range(3):
            part = None
            for d in range(3):
                rows = [xc[b, a + d : a + d + n] for a, n in slots]
                rows = rows[0] if len(rows) == 1 else jnp.concatenate(rows, axis=0)
                term = jnp.dot(
                    rows.reshape(rows.shape[0] * SLICE, CELLS), em[d * CELLS : (d + 1) * CELLS],
                    preferred_element_type=F32,
                )
                part = term if part is None else part + term
            blocks.append(part.astype(BF16))
        return blocks

    def mixed(x, sectors):
        for s in range(GROUPS):
            part = lax.dot_general(
                x, op[s * KG : (s + 1) * KG].reshape(KG * CELLS, FLAT), (((1,), (1,)), ((), ())),
                preferred_element_type=F32,
            ).astype(BF16)
            for k in range(KG):
                for n, t in enumerate(sectors):
                    mt[s * KG + k, :, t * CELLS : (t + 1) * CELLS] = part[
                        n * SLICE : (n + 1) * SLICE, k * CELLS : (k + 1) * CELLS
                    ]

    def grad_term(a, n):
        return jnp.dot(
            mt[:, :, a * CELLS : (a + n) * CELLS].reshape(K * SLICE, n * CELLS), gs[a : a + n].reshape(n * CELLS, CH),
            preferred_element_type=F32,
        )

    wait_vertical(forwards[0])
    for b, block in enumerate(windows(((1, 14),))):
        xt[:, b * ROWS * PITCH : (b + 1) * ROWS * PITCH] = block
    mixed(xt[...], range(1, 15))
    whole_wait(gs.at[pl.ds(0, 15)], g_r)
    dwp[...] = grad_term(1, 14)

    wait_vertical((ig_up, ig_down))
    total = mid[...] + lat_in[0].astype(F32) + lat_in[1].astype(F32)
    lon_out[0] = total[:, 0:COLS].astype(BF16)
    lon_out[1] = total[:, 2 * COLS : 3 * COLS].astype(BF16)
    mid[:, COLS : 2 * COLS] = total[:, COLS : 2 * COLS]
    ig_west = remote(lon_out.at[0], lon_in.at[1], igsend.at[2], igrecv.at[2], (lat, west))
    ig_east = remote(lon_out.at[1], lon_in.at[0], igsend.at[3], igrecv.at[3], (lat, east))
    for s in range(2):
        seams[s].wait_recv()
        start_vertical(forwards[1 + s])
    for pair in forwards[1:]:
        wait_vertical(pair)
    for b, block in enumerate(windows(((0, 1), (15, 1)))):
        xt[0 : 2 * SLICE, b * ROWS * PITCH : (b + 1) * ROWS * PITCH] = block
    mixed(xt[0 : 2 * SLICE, :], (0, 15))
    scale = 1.0 / math.sqrt(CELLS * 512)
    term = (dwp[...] + grad_term(0, 1) + grad_term(15, 1)) * scale
    term = term.reshape(K, SLICE, CH)

    wcs[...] = jnp.where(core == 0, term[:, :, HALF:CH], term[:, :, 0:HALF])
    w_copy = remote(wcs, wcr, wsem.at[0], wsem.at[1], partner)
    w_copy.start()
    keep_half = jnp.where(core == 0, term[:, :, 0:HALF], term[:, :, HALF:CH])
    w_copy.wait_recv()
    keep_half = keep_half + wcr[...]

    for s in range(GROUPS):
        zs[s] = keep_half[s * KG : (s + 1) * KG].astype(BF16)

        @pl.when(z4 != s)
        def _():
            slot = lax.rem(z4 - s + 4, 4) - 1
            remote(zs.at[s], zb.at[slot], z_s.at[s], z_r, z4_peer(s)).start()

    ig_west.start()
    ig_east.start()

    to_first = remote(xc.at[:, 0], sg.at[rank], sg_s.at[0], sg_r, (lat, zhi * 16))
    to_last = remote(xc.at[:, 17], sg.at[rank], sg_s.at[1], sg_r, (lat, zhi * 16 + 15))

    @pl.when(not_first)
    def _():
        to_first.start()
        to_east.wait_recv()
        start_vertical(verticals[1])

    @pl.when(not_last)
    def _():
        to_last.start()
        to_west.wait_recv()
        start_vertical(verticals[2])

    @pl.when(z4 < GROUPS)
    def _():
        whole_wait(zb, z_r)
        part = zs[z4].astype(F32)
        for d in range(3):
            part += zb[d].astype(F32)
        zg[zgroup] = part.astype(BF16)
        for d in range(1, 4):
            remote(
                zg.at[zgroup], zg.at[zgroup], zg_s, zg_r, zfar_peer(lax.rem(zgroup + d, 4))
            ).start()

    @pl.when(z4 < GROUPS)
    def _():
        whole_wait(zgd, zg_r)
        part = zg[0].astype(F32)
        for d in range(1, 4):
            part += zg[d].astype(F32)
        mine = pl.ds(z4 * KG, KG)
        fin[mine] = part.astype(BF16)
        for d in range(1, 4):
            remote(fin.at[mine], fin.at[mine], fin_s, fin_r.at[z4], z4_peer(lax.rem(z4 + d, 4))).start()

    parts = (pl.ds(0, 2 * KG), pl.ds(2 * KG, KG))
    for s in range(GROUPS):
        @pl.when(z4 != s)
        def _():
            whole_wait(fin.at[pl.ds(s * KG, KG)], fin_r.at[s])

        if s == 0:
            continue
        ks = parts[s - 1]
        for d in range(1, 16):
            remote(fin.at[ks], dwv.at[rank, ks], ag_s.at[s - 1], ag_r.at[s - 1], plane_peer(d)).start()
        dwv[rank, ks] = fin[ks]

    wait_vertical(verticals[0])

    def from_sectors(slot, cols):
        whole_wait(sg.at[pl.ds(0, 15)], sg_r)
        sg[rank] = xc[:, slot]
        for b in range(3):
            block = sg[:, b].reshape(CH, CELLS).astype(F32).T.astype(BF16)
            xh[b * ROWS : (b + 1) * ROWS, cols, :] = block.reshape(ROWS, COLS, CH)

    @pl.when(not_first)
    def _():
        wait_vertical(verticals[1])

    @pl.when(not_last)
    def _():
        wait_vertical(verticals[2])

    @pl.when(rank == 0)
    def _():
        from_sectors(0, wcols)

    @pl.when(rank == 15)
    def _():
        from_sectors(17, ecols)

    flat_x = xh[...].reshape(FLAT, CH)
    acc = jnp.zeros((CELLS, CH), F32)
    for s in range(GROUPS):
        m = jnp.dot(op[s * KG : (s + 1) * KG].reshape(KG * CELLS, FLAT), flat_x, preferred_element_type=F32)
        m = m.astype(BF16).reshape(KG, CELLS, CH)
        for k in range(KG):
            acc += lax.dot_general(m[k], wv[s * KG + k], (((1,), (1,)), ((), ())), preferred_element_type=F32)
    out_ref[...] = acc.astype(BF16).reshape(ROWS, COLS, CH)

    ig_east.wait_recv()
    ig_west.wait_recv()
    total = mid[:, COLS : 2 * COLS] + lon_in[0].astype(F32) + lon_in[1].astype(F32)
    ig_ref[...] = total.astype(BF16)

    half = pl.ds(pl.multiple_of(core * HALF, HALF), HALF)
    small_eye = eye[0:HALF, 0:HALF]
    tails = []
    for s, ks in enumerate(parts):
        whole_wait(dwv.at[pl.ds(0, 15), ks], ag_r.at[s])
        for k in range(ks.start, ks.start + ks.size):
            block = dwv[:, k].reshape(CH, HALF)
            part = lax.dot_general(small_eye, block, (((1,), (1,)), ((), ())), preferred_element_type=F32)
            dw_ref[k, half, :] = part.astype(BF16)
        c = remote(dw_ref.at[ks, half], dw_ref.at[ks, half], fw_s.at[s], fw_r.at[s], partner)
        c.start()
        tails.append(c)

    for s, ks in enumerate(parts):
        whole_wait(dwv.at[pl.ds(0, 15), ks], ag_s.at[s])

    for s in range(GROUPS):
        @pl.when(z4 != s)
        def _():
            whole_wait(zs.at[s], z_s.at[s])

    @pl.when(z4 < GROUPS)
    def _():
        whole_wait(zgd, zg_s)
        whole_wait(zgd, fin_s)

    whole_wait(xc.at[1, pl.ds(1, 15)], xa_s)
    whole_wait(gs.at[pl.ds(0, 15)], g_s)
    w_copy.wait_send()
    ig_east.wait_send()
    ig_west.wait_send()

    for c in seams:
        c.wait_send()

    def sent_vertical(pairs):
        @pl.when(has_up)
        def _():
            for pair in pairs:
                pair[0].wait_send()

        @pl.when(has_down)
        def _():
            for pair in pairs:
                pair[1].wait_send()

    sent_vertical(forwards + ((ig_up, ig_down), verticals[0]))

    @pl.when(not_first)
    def _():
        to_first.wait_send()
        to_west.wait_send()
        sent_vertical(verticals[1:2])

    @pl.when(not_last)
    def _():
        to_last.wait_send()
        to_east.wait_send()
        sent_vertical(verticals[2:3])

    for c in tails:
        c.wait()


def finish(out_ref, ig_ref, dw_ref, out_hbm, ig_hbm, dw_hbm, wide, sems):
    copies = [
        pltpu.make_async_copy(out_ref, out_hbm, sems.at[0]),
        pltpu.make_async_copy(ig_ref, ig_hbm, sems.at[1]),
    ]
    for c in copies:
        c.start()
    for k in range(K):
        wide[k] = dw_ref[k].astype(F32)
        c = pltpu.make_async_copy(wide.at[k], dw_hbm.at[k], sems.at[2 + k])
        c.start()
        copies.append(c)
    for c in copies:
        c.wait()


def on_device(inputs, out_grad, weight, kernel_basis, band_start, band_width, lon_reach):
    vmem = pl.BlockSpec(memory_space=pltpu.VMEM)
    hbm = pl.BlockSpec(memory_space=pltpu.HBM)
    dma = pltpu.SemaphoreType.DMA
    piece = (KG, SLICE, HALF)
    scratch = [
        pltpu.SMEM((ROWS,), jnp.int32),
        pltpu.SMEM((ROWS,), jnp.int32),
        pltpu.SMEM((ROWS,), jnp.int32),
        pltpu.VMEM((K, CH, CH), BF16),
        pltpu.VMEM((K, BAND, ROWS, LONW), BF16),
        pltpu.VMEM((BAND, ROWS, LONW), F32),
        pltpu.VMEM((BAND + 2, ROWS, 128), F32),
        pltpu.VMEM((BAND + 1, ROWS, 128), F32),
        pltpu.VMEM((K, CELLS, FLAT), BF16),
        pltpu.VMEM((EXT, PITCH, CH), BF16),
        pltpu.VMEM((CH, CELLS), BF16),
        pltpu.VMEM((3, 18, SLICE, CELLS), BF16),
        pltpu.VMEM((3 * CELLS, ROWS * PITCH), BF16),
        pltpu.VMEM((14 * SLICE, FLAT), BF16),
        pltpu.VMEM((16, CELLS, CH), BF16),
        pltpu.VMEM((K, SLICE, 16 * CELLS), BF16),
        pltpu.VMEM((CH, K * CELLS), BF16),
        pltpu.VMEM((ROWS, 3 * COLS, CH), F32),
        pltpu.VMEM((2, ROWS, 3 * COLS, CH), BF16),
        pltpu.VMEM((2, ROWS, 3 * COLS, CH), BF16),
        pltpu.VMEM((2, ROWS, COLS, CH), BF16),
        pltpu.VMEM((2, ROWS, COLS, CH), BF16),
        pltpu.VMEM((K * SLICE, CH), F32),
        pltpu.VMEM((K, SLICE, HALF), F32),
        pltpu.VMEM((K, SLICE, HALF), F32),
        pltpu.VMEM((GROUPS,) + piece, BF16),
        pltpu.VMEM((3,) + piece, BF16),
        pltpu.VMEM((4,) + piece, BF16),
        pltpu.VMEM((3,) + piece, BF16),
        pltpu.VMEM((K, SLICE, HALF), BF16),
        pltpu.VMEM((16, K, SLICE, HALF), BF16),
        pltpu.VMEM((16, 3, SLICE, CELLS), BF16),
        pltpu.VMEM((CH, CH), BF16),
        dma((7,)), dma((8,)), dma((8,)), dma, dma, dma((2,)), dma((2,)), dma((6,)), dma((6,)), dma, dma,
        dma((4,)), dma((4,)), dma((2,)),
        dma((3,)), dma, dma, dma, dma, dma((3,)), dma((2,)), dma((2,)), dma((2,)), dma((2,)),
        dma((2,)), dma,
    ]
    out, ig, dw = pl.pallas_call(
        kernel,
        out_shape=(
            jax.ShapeDtypeStruct((ROWS, COLS, CH), BF16),
            jax.ShapeDtypeStruct((ROWS, COLS, CH), BF16),
            jax.ShapeDtypeStruct((K, CH, CH), BF16),
        ),
        in_specs=[hbm] * 7,
        out_specs=(vmem, vmem, vmem),
        scratch_shapes=scratch,
        compiler_params=pltpu.CompilerParams(collective_id=0, has_side_effects=True, vmem_limit_bytes=56 << 20),
    )(
        inputs, out_grad.reshape(CELLS, CH), weight, kernel_basis.transpose(1, 2, 0, 3),
        band_start, band_width, lon_reach,
    )
    return pl.pallas_call(
        finish,
        out_shape=(
            jax.ShapeDtypeStruct((ROWS, COLS, CH), BF16),
            jax.ShapeDtypeStruct((ROWS, COLS, CH), BF16),
            jax.ShapeDtypeStruct((K, CH, CH), F32),
        ),
        in_specs=[vmem] * 3,
        out_specs=(hbm, hbm, hbm),
        scratch_shapes=[pltpu.VMEM((K, CH, CH), F32), dma((2 + K,))],
        compiler_params=pltpu.CompilerParams(vmem_limit_bytes=56 << 20),
    )(out, ig, dw)


def solution(mesh):
    placed = (
        P("lat", "lon", None),
        P("lat", "lon", None),
        P(),
        P("lat", None, None, None),
        P("lat"),
        P("lat"),
        P("lat"),
    )
    return jax.shard_map(
        on_device,
        mesh=mesh,
        in_specs=placed,
        out_specs=(P("lat", "lon", None), P("lat", "lon", None), P()),
        check_vma=False,
    )
```

time: 70.4 us -> 67.8 us (0.963)
  the two profiles are of different devices: /device:TPU:35 before, /device:TPU:1 now
where the time goes in v3:
time: 67.8 us; the launch traced here: 67.7 us
  Pallas kernels  67 us (99%)
    pallas_call x1, Pallas kernels, on_device(): pl.pallas_call(kernel, out_shape=(jax.ShapeDtypeStruct((ROWS, COLS, CH),...  64.1 us
    pallas_call x1, Pallas kernels, on_device(): pl.pallas_call(finish, out_shape=(jax.ShapeDtypeStruct((ROWS, COLS, CH),...  2.88 us

profile of v3, /device:TPU:1, one launch (start us, length us, event | category | flops | bytes accessed | tf_op | source)
XLA Modules:
  0.0 67.7 jit_solution(5119994493779269710)
XLA Ops:
  0.6 64.1 %shard_map.94 = (bf16[8,16,256]{2,1,0:T(8,128)(2,1)}, bf16[8,16,256]{2,1,0:T(8,128)(2,1)}, bf16[9,256,256]{2,1,0:T(8,128)(2,1)}) custom-call(bf16[8,16,256]{2,1,0:T(8,128)(2,1)} %x_ref.1, bf16[128,256]{1,0:T(8,128)(2,1)} %bitcast.3, bf16[9,256,256]{2,1,0:T(8,128)(2,1)} %w_ref.1, bf16[9,17,8,33]{3,2,1,0:T(8,128)(2,1)} %bitcast.2, s32[8]{0:T(128)} %start_ref.1, ...), custom_call_target="tpu_custom_call" | custom-call | tf_op jit(solution)/shard_map/pallas_call | solution.py:541
  64.8 2.9 %shard_map.95 = (bf16[8,16,256]{2,1,0:T(8,128)(2,1)}, bf16[8,16,256]{2,1,0:T(8,128)(2,1)}, f32[9,256,256]{2,1,0:T(8,128)}) custom-call(bf16[8,16,256]{2,1,0:T(8,128)(2,1)} %get-tuple-element.6.out_ref, bf16[8,16,256]{2,1,0:T(8,128)(2,1)} %get-tuple-element.7.ig_ref, bf16[9,256,256]{2,1,0:T(8,128)(2,1)} %get-tuple-element.8.dw_ref), custom_call_target="tpu_custom_call" | custom-call | tf_op jit(solution)/shard_map/pallas_call | solution.py:556

commit v4 on v3

--- a/solution.py
+++ b/solution.py
@@ -32,16 +32,18 @@
     x_ref, g_ref, w_ref, kb_ref, start_ref, width_ref, reach_ref,
     out_ref, ig_ref, dw_ref,
     start_v, width_v, reach_v, wv, kbv, mask, kbs, comb, op,
-    xh, xtc, xc, em, xt, gs, mt, mgt, mid, lat_out, lat_in, lon_out, lon_in, dwp,
-    wcs, wcr, zs, zb, zg, zgd, fin, dwv, sg, eye,
-    lsem, xsend, xrecv, xa_s, xa_r, seam_s, seam_r, fsend, frecv, g_s, g_r, igsend, igrecv, wsem,
-    z_s, z_r, zg_s, zg_r, fin_s, fin_r, ag_s, ag_r, fw_s, fw_r, sg_s, sg_r,
+    xh, xtc, xc, em, xt, gown, gs, mt, mgt, mid, lat_out, lat_in, lon_out, lon_in, dwp,
+    zs, zb, zg, zgd, fin, dwv, dwt, sg, eye, outv, igv,
+    lsem, xsend, xrecv, xa_s, xa_r, seam_s, seam_r, fsend, frecv, g_s, g_r, igsend, igrecv,
+    z_s, z_r, zg_s, zg_r, fin_s, fin_r, ag_s, ag_r, fw_s, fw_r, sg_s, sg_r, osem,
 ):
     lat, lon = lax.axis_index("lat"), lax.axis_index("lon")
     core = lax.rem(lat, 2)
     zlo = lat // 2
     zhi = lon // 16
     rank = lax.rem(lon, 16)
+    cgroup, ohalf = rank // 2, lax.rem(rank, 2)
+    slot = ohalf * 8 + cgroup
     z4 = lax.rem(zlo, 4)
     zgroup = zhi * 2 + zlo // 4
     up, down = lat - 1, lat + 1
@@ -53,10 +55,10 @@
     def plane_peer(d):
         return (lat, zhi * 16 + lax.rem(rank + d, 16))
 
-    other_half = (lat, (1 - zhi) * 16 + rank)
-
-    def z4_peer(t):
-        return ((zlo - z4 + t) * 2 + core, lon)
+    olon = (1 - zhi) * 16 + rank
+
+    def z4_peer(t, h):
+        return ((zlo - z4 + t) * 2 + h, lon)
 
     def zfar_peer(t):
         return (((t % 2) * 4 + z4) * 2 + core, (t // 2) * 16 + rank)
@@ -74,23 +76,24 @@
         pltpu.make_async_copy(start_ref, start_v, lsem.at[1]),
         pltpu.make_async_copy(width_ref, width_v, lsem.at[2]),
         pltpu.make_async_copy(reach_ref, reach_v, lsem.at[3]),
-        pltpu.make_async_copy(g_ref, gs.at[rank], lsem.at[4]),
+        pltpu.make_async_copy(g_ref.at[:, pl.ds(0, HALF)], gown.at[0], lsem.at[4]),
         pltpu.make_async_copy(w_ref, wv, lsem.at[5]),
         pltpu.make_async_copy(x_ref, xh.at[mid_rows, mid_cols], lsem.at[6]),
+        pltpu.make_async_copy(g_ref.at[:, pl.ds(HALF, HALF)], gown.at[1], lsem.at[7]),
     ]
-    for c in (local[6],) + tuple(local[:6]):
+    for c in (local[6],) + tuple(local[:6]) + (local[7],):
         c.start()
 
     @pl.when(jnp.logical_not(has_up))
     def _():
         xh[0:ROWS] = jnp.zeros((ROWS, PITCH, CH), BF16)
-        xc[0] = jnp.zeros((18, SLICE, CELLS), BF16)
+        xc[0] = jnp.zeros((18, 2, SLICE, CELLS), BF16)
         lat_in[0] = jnp.zeros((ROWS, 3 * COLS, CH), BF16)
 
     @pl.when(jnp.logical_not(has_down))
     def _():
         xh[2 * ROWS : EXT] = jnp.zeros((ROWS, PITCH, CH), BF16)
-        xc[2] = jnp.zeros((18, SLICE, CELLS), BF16)
+        xc[2] = jnp.zeros((18, 2, SLICE, CELLS), BF16)
         lat_in[1] = jnp.zeros((ROWS, 3 * COLS, CH), BF16)
 
     bar = pltpu.get_barrier_semaphore()
@@ -103,20 +106,26 @@
     for d in range(1, 16):
         signal(plane_peer(d))
     for d in range(1, 4):
-        signal(z4_peer(lax.rem(z4 + d, 4)))
+        for h in range(2):
+            signal(z4_peer(lax.rem(z4 + d, 4), h))
 
     @pl.when(has_up)
     def _():
+        signal((up, olon))
         signal((up, lon))
 
     @pl.when(has_down)
     def _():
+        signal((down, olon))
         signal((down, lon))
 
     local[6].wait()
-    xtc[...] = xh[mid_rows, mid_cols, :].reshape(CELLS, CH).astype(F32).T.astype(BF16)
-    own = pl.ds(pl.multiple_of(rank * SLICE, SLICE), SLICE)
-    xc[1, 1 + rank] = xtc[own, :]
+    xtc[...] = xh[mid_rows, mid_cols, :].reshape(CELLS, CH).astype(F32).T.astype(BF16).reshape(2, HALF, CELLS)
+
+    def channels(group):
+        return pl.ds(pl.multiple_of(group * SLICE, SLICE), SLICE)
+
+    xc[1, 1 + rank] = xtc[:, channels(cgroup), :]
 
     kbs[...] = jnp.zeros_like(kbs)
     xh[:, 3 * COLS : PITCH] = jnp.zeros((EXT, PITCH - 3 * COLS, CH), BF16)
@@ -156,15 +165,18 @@
 
     lax.fori_loop(0, K, op_step, 0)
 
-    pl.semaphore_wait(bar, 21 + has_up.astype(jnp.int32) + has_down.astype(jnp.int32))
-
+    pl.semaphore_wait(bar, 24 + 2 * (has_up.astype(jnp.int32) + has_down.astype(jnp.int32)))
+
+    which = jnp.where(rank == 0, 0, jnp.where(rank == 15, 1, 2))
     for d in range(1, 16):
-        peer_rows = pl.ds(pl.multiple_of(lax.rem(rank + d, 16) * SLICE, SLICE), SLICE)
-        remote(xtc.at[peer_rows], xc.at[1, 1 + rank], xa_s, xa_r, plane_peer(d)).start()
+        peer = lax.rem(rank + d, 16)
+        remote(xtc.at[:, channels(peer // 2), :], xc.at[1, 1 + rank], xa_s, xa_r.at[which], plane_peer(d)).start()
     local[4].wait()
+    local[7].wait()
+    gs[rank] = gown[ohalf]
     for d in range(1, 16):
-        remote(gs.at[rank], gs.at[rank], g_s, g_r, plane_peer(d)).start()
-
+        peer = lax.rem(rank + d, 16)
+        remote(gown.at[lax.rem(peer, 2)], gs.at[rank], g_s, g_r, plane_peer(d)).start()
 
     def start_vertical(pair):
         @pl.when(has_up)
@@ -191,14 +203,40 @@
             remote(src, xc.at[0, slots], fsend.at[s + 1], frecv.at[s + 1], (down, lon)),
         )
 
-    forwards = (forward(pl.ds(1, 16), 0), forward(pl.ds(0, 1), 2), forward(pl.ds(17, 1), 4))
-    whole_wait(xc.at[1, pl.ds(1, 15)], xa_r)
-    seams = (
-        remote(xc.at[1, 16], xc.at[1, 0], seam_s.at[0], seam_r.at[0], other_half),
-        remote(xc.at[1, 1], xc.at[1, 17], seam_s.at[1], seam_r.at[1], other_half),
-    )
-    for c in seams:
-        c.start()
+    def seam(src_slot, dst_slot, n):
+        src = xc.at[1, src_slot]
+        return (
+            remote(src, xc.at[2, dst_slot], seam_s.at[n], seam_r.at[n], (up, olon)),
+            remote(src, xc.at[0, dst_slot], seam_s.at[n + 1], seam_r.at[n + 1], (down, olon)),
+            remote(src, xc.at[1, dst_slot], seam_s.at[n + 2], seam_r.at[n + 2], (lat, olon)),
+        )
+
+    seams = (seam(16, 0, 0), seam(1, 17, 3))
+    forwards = (forward(pl.ds(1, 16), 0),)
+
+    @pl.when(not_first)
+    def _():
+        whole_wait(xc.at[1, 1], xa_r.at[0])
+
+    start_vertical(seams[1])
+    seams[1][2].start()
+
+    @pl.when(not_last)
+    def _():
+        whole_wait(xc.at[1, 16], xa_r.at[1])
+
+    start_vertical(seams[0])
+    seams[0][2].start()
+    at_end = jnp.logical_or(rank == 0, rank == 15)
+
+    @pl.when(at_end)
+    def _():
+        whole_wait(xc.at[1, pl.ds(1, 14)], xa_r.at[2])
+
+    @pl.when(jnp.logical_not(at_end))
+    def _():
+        whole_wait(xc.at[1, pl.ds(1, 13)], xa_r.at[2])
+
     start_vertical(forwards[0])
 
     to_east = remote(x_ref, xh.at[mid_rows, wcols], xsend.at[0], xrecv.at[0], (lat, east))
@@ -213,7 +251,7 @@
         to_west.start()
 
     local[5].wait()
-    g = gs[rank]
+    g = jnp.concatenate([gown[0], gown[1]], axis=1)
 
     for k in range(K):
         part = jnp.dot(g, wv[k], preferred_element_type=F32).astype(BF16)
@@ -255,7 +293,7 @@
                 rows = [xc[b, a + d : a + d + n] for a, n in slots]
                 rows = rows[0] if len(rows) == 1 else jnp.concatenate(rows, axis=0)
                 term = jnp.dot(
-                    rows.reshape(rows.shape[0] * SLICE, CELLS), em[d * CELLS : (d + 1) * CELLS],
+                    rows.reshape(rows.shape[0] * 2 * SLICE, CELLS), em[d * CELLS : (d + 1) * CELLS],
                     preferred_element_type=F32,
                 )
                 part = term if part is None else part + term
@@ -271,12 +309,13 @@
             for k in range(KG):
                 for n, t in enumerate(sectors):
                     mt[s * KG + k, :, t * CELLS : (t + 1) * CELLS] = part[
-                        n * SLICE : (n + 1) * SLICE, k * CELLS : (k + 1) * CELLS
+                        n * 2 * SLICE : (n + 1) * 2 * SLICE, k * CELLS : (k + 1) * CELLS
                     ]
 
     def grad_term(a, n):
         return jnp.dot(
-            mt[:, :, a * CELLS : (a + n) * CELLS].reshape(K * SLICE, n * CELLS), gs[a : a + n].reshape(n * CELLS, CH),
+            mt[:, :, a * CELLS : (a + n) * CELLS].reshape(K * 2 * SLICE, n * CELLS),
+            gs[a : a + n].reshape(n * CELLS, HALF),
             preferred_element_type=F32,
         )
 
@@ -294,38 +333,30 @@
     mid[:, COLS : 2 * COLS] = total[:, COLS : 2 * COLS]
     ig_west = remote(lon_out.at[0], lon_in.at[1], igsend.at[2], igrecv.at[2], (lat, west))
     ig_east = remote(lon_out.at[1], lon_in.at[0], igsend.at[3], igrecv.at[3], (lat, east))
-    for s in range(2):
-        seams[s].wait_recv()
-        start_vertical(forwards[1 + s])
-    for pair in forwards[1:]:
-        wait_vertical(pair)
+    for trio in seams:
+        trio[2].wait_recv()
+        wait_vertical(trio)
     for b, block in enumerate(windows(((0, 1), (15, 1)))):
-        xt[0 : 2 * SLICE, b * ROWS * PITCH : (b + 1) * ROWS * PITCH] = block
-    mixed(xt[0 : 2 * SLICE, :], (0, 15))
+        xt[0 : 4 * SLICE, b * ROWS * PITCH : (b + 1) * ROWS * PITCH] = block
+    mixed(xt[0 : 4 * SLICE, :], (0, 15))
     scale = 1.0 / math.sqrt(CELLS * 512)
     term = (dwp[...] + grad_term(0, 1) + grad_term(15, 1)) * scale
-    term = term.reshape(K, SLICE, CH)
-
-    wcs[...] = jnp.where(core == 0, term[:, :, HALF:CH], term[:, :, 0:HALF])
-    w_copy = remote(wcs, wcr, wsem.at[0], wsem.at[1], partner)
-    w_copy.start()
-    keep_half = jnp.where(core == 0, term[:, :, 0:HALF], term[:, :, HALF:CH])
-    w_copy.wait_recv()
-    keep_half = keep_half + wcr[...]
+    term = term.reshape(K, 2, SLICE, HALF)
 
     for s in range(GROUPS):
-        zs[s] = keep_half[s * KG : (s + 1) * KG].astype(BF16)
-
-        @pl.when(z4 != s)
-        def _():
-            slot = lax.rem(z4 - s + 4, 4) - 1
-            remote(zs.at[s], zb.at[slot], z_s.at[s], z_r, z4_peer(s)).start()
+        for h in range(2):
+            zs[s, h] = term[s * KG : (s + 1) * KG, h].astype(BF16)
+
+            @pl.when(jnp.logical_or(z4 != s, core != h))
+            def _():
+                place = lax.rem(z4 - s + 4, 4) * 2 + lax.rem(core - h + 2, 2) - 1
+                remote(zs.at[s, h], zb.at[place], z_s.at[2 * s + h], z_r, z4_peer(s, h)).start()
 
     ig_west.start()
     ig_east.start()
 
-    to_first = remote(xc.at[:, 0], sg.at[rank], sg_s.at[0], sg_r, (lat, zhi * 16))
-    to_last = remote(xc.at[:, 17], sg.at[rank], sg_s.at[1], sg_r, (lat, zhi * 16 + 15))
+    to_first = remote(xc.at[:, 0, ohalf], sg.at[slot], sg_s.at[0], sg_r, (lat, zhi * 16))
+    to_last = remote(xc.at[:, 17, ohalf], sg.at[slot], sg_s.at[1], sg_r, (lat, zhi * 16 + 15))
 
     @pl.when(not_first)
     def _():
@@ -342,8 +373,8 @@
     @pl.when(z4 < GROUPS)
     def _():
         whole_wait(zb, z_r)
-        part = zs[z4].astype(F32)
-        for d in range(3):
+        part = zs[z4, core].astype(F32)
+        for d in range(7):
             part += zb[d].astype(F32)
         zg[zgroup] = part.astype(BF16)
         for d in range(1, 4):
@@ -360,7 +391,7 @@
         mine = pl.ds(z4 * KG, KG)
         fin[mine] = part.astype(BF16)
         for d in range(1, 4):
-            remote(fin.at[mine], fin.at[mine], fin_s, fin_r.at[z4], z4_peer(lax.rem(z4 + d, 4))).start()
+            remote(fin.at[mine], fin.at[mine], fin_s, fin_r.at[z4], z4_peer(lax.rem(z4 + d, 4), core)).start()
 
     parts = (pl.ds(0, 2 * KG), pl.ds(2 * KG, KG))
     for s in range(GROUPS):
@@ -372,14 +403,14 @@
             continue
         ks = parts[s - 1]
         for d in range(1, 16):
-            remote(fin.at[ks], dwv.at[rank, ks], ag_s.at[s - 1], ag_r.at[s - 1], plane_peer(d)).start()
-        dwv[rank, ks] = fin[ks]
+            remote(fin.at[ks], dwv.at[slot, ks], ag_s.at[s - 1], ag_r.at[s - 1], plane_peer(d)).start()
+        dwv[slot, ks] = fin[ks]
 
     wait_vertical(verticals[0])
 
-    def from_sectors(slot, cols):
+    def from_sectors(sector, cols):
         whole_wait(sg.at[pl.ds(0, 15)], sg_r)
-        sg[rank] = xc[:, slot]
+        sg[slot] = xc[:, sector, ohalf]
         for b in range(3):
             block = sg[:, b].reshape(CH, CELLS).astype(F32).T.astype(BF16)
             xh[b * ROWS : (b + 1) * ROWS, cols, :] = block.reshape(ROWS, COLS, CH)
@@ -407,33 +438,39 @@
         m = m.astype(BF16).reshape(KG, CELLS, CH)
         for k in range(KG):
             acc += lax.dot_general(m[k], wv[s * KG + k], (((1,), (1,)), ((), ())), preferred_element_type=F32)
-    out_ref[...] = acc.astype(BF16).reshape(ROWS, COLS, CH)
+    outv[...] = acc.astype(BF16).reshape(ROWS, COLS, CH)
+    tails = [pltpu.make_async_copy(outv, out_ref, osem.at[0])]
+    tails[0].start()
 
     ig_east.wait_recv()
     ig_west.wait_recv()
     total = mid[:, COLS : 2 * COLS] + lon_in[0].astype(F32) + lon_in[1].astype(F32)
-    ig_ref[...] = total.astype(BF16)
+    igv[...] = total.astype(BF16)
+    tails.append(pltpu.make_async_copy(igv, ig_ref, osem.at[1]))
+    tails[1].start()
 
     half = pl.ds(pl.multiple_of(core * HALF, HALF), HALF)
     small_eye = eye[0:HALF, 0:HALF]
-    tails = []
     for s, ks in enumerate(parts):
         whole_wait(dwv.at[pl.ds(0, 15), ks], ag_r.at[s])
         for k in range(ks.start, ks.start + ks.size):
-            block = dwv[:, k].reshape(CH, HALF)
-            part = lax.dot_general(small_eye, block, (((1,), (1,)), ((), ())), preferred_element_type=F32)
-            dw_ref[k, half, :] = part.astype(BF16)
-        c = remote(dw_ref.at[ks, half], dw_ref.at[ks, half], fw_s.at[s], fw_r.at[s], partner)
-        c.start()
-        tails.append(c)
+            for h in range(2):
+                block = dwv[8 * h : 8 * h + 8, k].reshape(HALF, HALF)
+                part = lax.dot_general(small_eye, block, (((1,), (1,)), ((), ())), preferred_element_type=F32)
+                dwt[k, h * HALF : (h + 1) * HALF, :] = part.astype(BF16)
+        tails.append(remote(dwt.at[ks], dw_ref.at[ks, :, half], fw_s.at[s], fw_r.at[s], partner))
+        tails.append(pltpu.make_async_copy(dwt.at[ks], dw_ref.at[ks, :, half], osem.at[2 + s]))
+        tails[-2].start()
+        tails[-1].start()
 
     for s, ks in enumerate(parts):
         whole_wait(dwv.at[pl.ds(0, 15), ks], ag_s.at[s])
 
     for s in range(GROUPS):
-        @pl.when(z4 != s)
-        def _():
-            whole_wait(zs.at[s], z_s.at[s])
+        for h in range(2):
+            @pl.when(jnp.logical_or(z4 != s, core != h))
+            def _():
+                whole_wait(zs.at[s, h], z_s.at[2 * s + h])
 
     @pl.when(z4 < GROUPS)
     def _():
@@ -442,12 +479,11 @@
 
     whole_wait(xc.at[1, pl.ds(1, 15)], xa_s)
     whole_wait(gs.at[pl.ds(0, 15)], g_s)
-    w_copy.wait_send()
     ig_east.wait_send()
     ig_west.wait_send()
 
-    for c in seams:
-        c.wait_send()
+    for trio in seams:
+        trio[2].wait_send()
 
     def sent_vertical(pairs):
         @pl.when(has_up)
@@ -460,7 +496,7 @@
             for pair in pairs:
                 pair[1].wait_send()
 
-    sent_vertical(forwards + ((ig_up, ig_down), verticals[0]))
+    sent_vertical(forwards + seams + ((ig_up, ig_down), verticals[0]))
 
     @pl.when(not_first)
     def _():
@@ -478,24 +514,29 @@
         c.wait()
 
 
-def finish(out_ref, ig_ref, dw_ref, out_hbm, ig_hbm, dw_hbm, wide, sems):
-    copies = [
-        pltpu.make_async_copy(out_ref, out_hbm, sems.at[0]),
-        pltpu.make_async_copy(ig_ref, ig_hbm, sems.at[1]),
+def finish(out_ref, ig_ref, dw_ref, out_hbm, ig_hbm, dw_hbm, small, narrow, wide, sems):
+    loads = [pltpu.make_async_copy(dw_ref.at[k], narrow.at[k], sems.at[k]) for k in range(K)]
+    loads += [
+        pltpu.make_async_copy(out_ref, small.at[0], sems.at[K]),
+        pltpu.make_async_copy(ig_ref, small.at[1], sems.at[K + 1]),
     ]
-    for c in copies:
+    stores = [pltpu.make_async_copy(wide.at[k], dw_hbm.at[k], sems.at[K + 2 + k]) for k in range(K)]
+    stores += [
+        pltpu.make_async_copy(small.at[0], out_hbm, sems.at[2 * K + 2]),
+        pltpu.make_async_copy(small.at[1], ig_hbm, sems.at[2 * K + 3]),
+    ]
+    for c in loads:
         c.start()
-    for k in range(K):
-        wide[k] = dw_ref[k].astype(F32)
-        c = pltpu.make_async_copy(wide.at[k], dw_hbm.at[k], sems.at[2 + k])
-        c.start()
-        copies.append(c)
-    for c in copies:
+    for k in range(K + 2):
+        loads[k].wait()
+        if k < K:
+            wide[k] = narrow[k].astype(F32)
+        stores[k].start()
+    for c in stores:
         c.wait()
 
 
 def on_device(inputs, out_grad, weight, kernel_basis, band_start, band_width, lon_reach):
-    vmem = pl.BlockSpec(memory_space=pltpu.VMEM)
     hbm = pl.BlockSpec(memory_space=pltpu.HBM)
     dma = pltpu.SemaphoreType.DMA
     piece = (KG, SLICE, HALF)
@@ -510,33 +551,34 @@
         pltpu.VMEM((BAND + 1, ROWS, 128), F32),
         pltpu.VMEM((K, CELLS, FLAT), BF16),
         pltpu.VMEM((EXT, PITCH, CH), BF16),
-        pltpu.VMEM((CH, CELLS), BF16),
-        pltpu.VMEM((3, 18, SLICE, CELLS), BF16),
+        pltpu.VMEM((2, HALF, CELLS), BF16),
+        pltpu.VMEM((3, 18, 2, SLICE, CELLS), BF16),
         pltpu.VMEM((3 * CELLS, ROWS * PITCH), BF16),
-        pltpu.VMEM((14 * SLICE, FLAT), BF16),
-        pltpu.VMEM((16, CELLS, CH), BF16),
-        pltpu.VMEM((K, SLICE, 16 * CELLS), BF16),
+        pltpu.VMEM((28 * SLICE, FLAT), BF16),
+        pltpu.VMEM((2, CELLS, HALF), BF16),
+        pltpu.VMEM((16, CELLS, HALF), BF16),
+        pltpu.VMEM((K, 2 * SLICE, 16 * CELLS), BF16),
         pltpu.VMEM((CH, K * CELLS), BF16),
         pltpu.VMEM((ROWS, 3 * COLS, CH), F32),
         pltpu.VMEM((2, ROWS, 3 * COLS, CH), BF16),
         pltpu.VMEM((2, ROWS, 3 * COLS, CH), BF16),
         pltpu.VMEM((2, ROWS, COLS, CH), BF16),
         pltpu.VMEM((2, ROWS, COLS, CH), BF16),
-        pltpu.VMEM((K * SLICE, CH), F32),
-        pltpu.VMEM((K, SLICE, HALF), F32),
-        pltpu.VMEM((K, SLICE, HALF), F32),
-        pltpu.VMEM((GROUPS,) + piece, BF16),
-        pltpu.VMEM((3,) + piece, BF16),
+        pltpu.VMEM((K * 2 * SLICE, HALF), F32),
+        pltpu.VMEM((GROUPS, 2) + piece, BF16),
+        pltpu.VMEM((7,) + piece, BF16),
         pltpu.VMEM((4,) + piece, BF16),
         pltpu.VMEM((3,) + piece, BF16),
         pltpu.VMEM((K, SLICE, HALF), BF16),
         pltpu.VMEM((16, K, SLICE, HALF), BF16),
+        pltpu.VMEM((K, CH, HALF), BF16),
         pltpu.VMEM((16, 3, SLICE, CELLS), BF16),
         pltpu.VMEM((CH, CH), BF16),
-        dma((7,)), dma((8,)), dma((8,)), dma, dma, dma((2,)), dma((2,)), dma((6,)), dma((6,)), dma, dma,
-        dma((4,)), dma((4,)), dma((2,)),
-        dma((3,)), dma, dma, dma, dma, dma((3,)), dma((2,)), dma((2,)), dma((2,)), dma((2,)),
-        dma((2,)), dma,
+        pltpu.VMEM((ROWS, COLS, CH), BF16),
+        pltpu.VMEM((ROWS, COLS, CH), BF16),
+        dma((8,)), dma((8,)), dma((8,)), dma, dma((3,)), dma((6,)), dma((6,)), dma((2,)), dma((2,)), dma, dma,
+        dma((4,)), dma((4,)),
+        dma((6,)), dma, dma, dma, dma, dma((3,)), dma((2,)), dma((2,)), dma((2,)), dma((2,)), dma((2,)), dma, dma((4,)),
     ]
     out, ig, dw = pl.pallas_call(
         kernel,
@@ -546,7 +588,7 @@
             jax.ShapeDtypeStruct((K, CH, CH), BF16),
         ),
         in_specs=[hbm] * 7,
-        out_specs=(vmem, vmem, vmem),
+        out_specs=(hbm, hbm, hbm),
         scratch_shapes=scratch,
         compiler_params=pltpu.CompilerParams(collective_id=0, has_side_effects=True, vmem_limit_bytes=56 << 20),
     )(
@@ -560,9 +602,14 @@
             jax.ShapeDtypeStruct((ROWS, COLS, CH), BF16),
             jax.ShapeDtypeStruct((K, CH, CH), F32),
         ),
-        in_specs=[vmem] * 3,
+        in_specs=[hbm] * 3,
         out_specs=(hbm, hbm, hbm),
-        scratch_shapes=[pltpu.VMEM((K, CH, CH), F32), dma((2 + K,))],
+        scratch_shapes=[
+            pltpu.VMEM((2, ROWS, COLS, CH), BF16),
+            pltpu.VMEM((K, CH, CH), BF16),
+            pltpu.VMEM((K, CH, CH), F32),
+            dma((2 * K + 4,)),
+        ],
         compiler_params=pltpu.CompilerParams(vmem_limit_bytes=56 << 20),
     )(out, ig, dw)
 

time: 67.8 us -> 63 us (0.929)
  Pallas kernels: 67 us -> 61.9 us
    pallas_call x1, Pallas kernels: 64.1 us -> 59.4 us  [on_device(): pl.pallas_call(kernel, out_shape=(jax.ShapeDtypeStruct((ROWS, COLS, CH),...]
where the time goes in v4:
time: 63 us; the launch traced here: 62.6 us
  Pallas kernels  61.9 us (98%)
  between operations  0.64 us (1%)
    pallas_call x1, Pallas kernels, on_device(): pl.pallas_call(kernel, out_shape=(jax.ShapeDtypeStruct((ROWS, COLS, CH),...  59.4 us
    pallas_call x1, Pallas kernels, on_device(): pl.pallas_call(finish, out_shape=(jax.ShapeDtypeStruct((ROWS, COLS, CH),...  2.54 us

profile of v4, /device:TPU:1, one launch (start us, length us, event | category | flops | bytes accessed | tf_op | source)
XLA Modules:
  0.0 62.6 jit_solution(1641645544844385364)
XLA Ops:
  0.6 59.4 %shard_map.94 = (bf16[8,16,256]{2,1,0:T(8,128)(2,1)}, bf16[8,16,256]{2,1,0:T(8,128)(2,1)}, bf16[9,256,256]{2,1,0:T(8,128)(2,1)}) custom-call(bf16[8,16,256]{2,1,0:T(8,128)(2,1)} %x_ref.1, bf16[128,256]{1,0:T(8,128)(2,1)} %bitcast.3, bf16[9,256,256]{2,1,0:T(8,128)(2,1)} %w_ref.1, bf16[9,17,8,33]{3,2,1,0:T(8,128)(2,1)} %bitcast.2, s32[8]{0:T(128)} %start_ref.1, ...), custom_call_target="tpu_custom_call" | custom-call | tf_op jit(solution)/shard_map/pallas_call | solution.py:583
  60.0 2.5 %shard_map.95 = (bf16[8,16,256]{2,1,0:T(8,128)(2,1)}, bf16[8,16,256]{2,1,0:T(8,128)(2,1)}, f32[9,256,256]{2,1,0:T(8,128)}) custom-call(bf16[8,16,256]{2,1,0:T(8,128)(2,1)} %get-tuple-element.6.out_ref, bf16[8,16,256]{2,1,0:T(8,128)(2,1)} %get-tuple-element.7.ig_ref, bf16[9,256,256]{2,1,0:T(8,128)(2,1)} %get-tuple-element.8.dw_ref), custom_call_target="tpu_custom_call" | custom-call | tf_op jit(solution)/shard_map/pallas_call | solution.py:598

commit v5 on v4

--- a/solution.py
+++ b/solution.py
@@ -20,6 +20,9 @@
 PAIRS = EXT // 2
 HALF = 128
 GROUPS = 3
+OWNERS = 4
+FINAL = ((0, 3), (3, 5), (5, 7), (7, 9))
+REST = (((3, 7), (7, 9)), ((0, 3), (5, 9)), ((0, 5), (7, 9)), ((0, 4), (4, 7)))
 KG = K // GROUPS
 SLICE = 16
 
@@ -33,9 +36,9 @@
     out_ref, ig_ref, dw_ref,
     start_v, width_v, reach_v, wv, kbv, mask, kbs, comb, op,
     xh, xtc, xc, em, xt, gown, gs, mt, mgt, mid, lat_out, lat_in, lon_out, lon_in, dwp,
-    zs, zb, zg, zgd, fin, dwv, dwt, sg, eye, outv, igv,
+    zs, zb, zg, zgd, finb, fin, dwv, sg, eye,
     lsem, xsend, xrecv, xa_s, xa_r, seam_s, seam_r, fsend, frecv, g_s, g_r, igsend, igrecv,
-    z_s, z_r, zg_s, zg_r, fin_s, fin_r, ag_s, ag_r, fw_s, fw_r, sg_s, sg_r, osem,
+    z_s, z_r, zg_s, zg_r, fin_s, fin_r, ag_s, ag_r, fw_s, fw_r, sg_s, sg_r,
 ):
     lat, lon = lax.axis_index("lat"), lax.axis_index("lon")
     core = lax.rem(lat, 2)
@@ -343,9 +346,9 @@
     term = (dwp[...] + grad_term(0, 1) + grad_term(15, 1)) * scale
     term = term.reshape(K, 2, SLICE, HALF)
 
-    for s in range(GROUPS):
+    for s in range(OWNERS):
         for h in range(2):
-            zs[s, h] = term[s * KG : (s + 1) * KG, h].astype(BF16)
+            zs[s, h] = term[2 * s : 2 * s + KG, h].astype(BF16)
 
             @pl.when(jnp.logical_or(z4 != s, core != h))
             def _():
@@ -370,41 +373,45 @@
         to_west.wait_recv()
         start_vertical(verticals[2])
 
-    @pl.when(z4 < GROUPS)
-    def _():
-        whole_wait(zb, z_r)
-        part = zs[z4, core].astype(F32)
-        for d in range(7):
-            part += zb[d].astype(F32)
-        zg[zgroup] = part.astype(BF16)
-        for d in range(1, 4):
-            remote(
-                zg.at[zgroup], zg.at[zgroup], zg_s, zg_r, zfar_peer(lax.rem(zgroup + d, 4))
-            ).start()
-
-    @pl.when(z4 < GROUPS)
-    def _():
-        whole_wait(zgd, zg_r)
-        part = zg[0].astype(F32)
-        for d in range(1, 4):
-            part += zg[d].astype(F32)
-        mine = pl.ds(z4 * KG, KG)
-        fin[mine] = part.astype(BF16)
-        for d in range(1, 4):
-            remote(fin.at[mine], fin.at[mine], fin_s, fin_r.at[z4], z4_peer(lax.rem(z4 + d, 4), core)).start()
-
-    parts = (pl.ds(0, 2 * KG), pl.ds(2 * KG, KG))
-    for s in range(GROUPS):
+    whole_wait(zb, z_r)
+    part = zs[z4, core].astype(F32)
+    for d in range(7):
+        part += zb[d].astype(F32)
+    zg[zgroup] = part.astype(BF16)
+    for d in range(1, 4):
+        remote(zg.at[zgroup], zg.at[zgroup], zg_s, zg_r, zfar_peer(lax.rem(zgroup + d, 4))).start()
+
+    whole_wait(zgd, zg_r)
+    part = zg[0].astype(F32)
+    for d in range(1, 4):
+        part += zg[d].astype(F32)
+    finb[z4] = part.astype(BF16)
+
+    def gather(lo, hi, n):
+        ks = pl.ds(lo, hi - lo)
+        for d in range(1, 16):
+            remote(fin.at[ks], dwv.at[slot, ks], ag_s.at[n], ag_r.at[n], plane_peer(d)).start()
+        dwv[slot, ks] = fin[ks]
+
+    for d in range(1, 4):
+        remote(finb.at[z4], finb.at[z4], fin_s, fin_r.at[z4], z4_peer(lax.rem(z4 + d, 4), core)).start()
+    for s, (lo, hi) in enumerate(FINAL):
+        @pl.when(z4 == s)
+        def _():
+            fin[lo:hi] = finb[s, lo - 2 * s : hi - 2 * s]
+            gather(lo, hi, 0)
+
+    for s, (lo, hi) in enumerate(FINAL):
         @pl.when(z4 != s)
         def _():
-            whole_wait(fin.at[pl.ds(s * KG, KG)], fin_r.at[s])
-
-        if s == 0:
-            continue
-        ks = parts[s - 1]
-        for d in range(1, 16):
-            remote(fin.at[ks], dwv.at[slot, ks], ag_s.at[s - 1], ag_r.at[s - 1], plane_peer(d)).start()
-        dwv[slot, ks] = fin[ks]
+            whole_wait(finb.at[s], fin_r.at[s])
+            fin[lo:hi] = finb[s, lo - 2 * s : hi - 2 * s]
+
+    for s in range(OWNERS):
+        @pl.when(z4 == s)
+        def _():
+            for n, (lo, hi) in enumerate(REST[s]):
+                gather(lo, hi, 1 + n)
 
     wait_vertical(verticals[0])
 
@@ -438,44 +445,39 @@
         m = m.astype(BF16).reshape(KG, CELLS, CH)
         for k in range(KG):
             acc += lax.dot_general(m[k], wv[s * KG + k], (((1,), (1,)), ((), ())), preferred_element_type=F32)
-    outv[...] = acc.astype(BF16).reshape(ROWS, COLS, CH)
-    tails = [pltpu.make_async_copy(outv, out_ref, osem.at[0])]
-    tails[0].start()
+    out_ref[...] = acc.astype(BF16).reshape(ROWS, COLS, CH)
 
     ig_east.wait_recv()
     ig_west.wait_recv()
     total = mid[:, COLS : 2 * COLS] + lon_in[0].astype(F32) + lon_in[1].astype(F32)
-    igv[...] = total.astype(BF16)
-    tails.append(pltpu.make_async_copy(igv, ig_ref, osem.at[1]))
-    tails[1].start()
-
-    half = pl.ds(pl.multiple_of(core * HALF, HALF), HALF)
+    ig_ref[...] = total.astype(BF16)
+
     small_eye = eye[0:HALF, 0:HALF]
-    for s, ks in enumerate(parts):
-        whole_wait(dwv.at[pl.ds(0, 15), ks], ag_r.at[s])
-        for k in range(ks.start, ks.start + ks.size):
-            for h in range(2):
-                block = dwv[8 * h : 8 * h + 8, k].reshape(HALF, HALF)
-                part = lax.dot_general(small_eye, block, (((1,), (1,)), ((), ())), preferred_element_type=F32)
-                dwt[k, h * HALF : (h + 1) * HALF, :] = part.astype(BF16)
-        tails.append(remote(dwt.at[ks], dw_ref.at[ks, :, half], fw_s.at[s], fw_r.at[s], partner))
-        tails.append(pltpu.make_async_copy(dwt.at[ks], dw_ref.at[ks, :, half], osem.at[2 + s]))
-        tails[-2].start()
-        tails[-1].start()
-
-    for s, ks in enumerate(parts):
-        whole_wait(dwv.at[pl.ds(0, 15), ks], ag_s.at[s])
-
-    for s in range(GROUPS):
+
+    def hand_over(lo, hi, n):
+        ks = pl.ds(lo, hi - lo)
+        return remote(dw_ref.at[core, ks], dw_ref.at[core, ks], fw_s.at[n], fw_r.at[n], partner)
+
+    for s in range(OWNERS):
+        @pl.when(z4 == s)
+        def _():
+            for n, (lo, hi) in enumerate((FINAL[s],) + REST[s]):
+                whole_wait(dwv.at[pl.ds(0, 15), pl.ds(lo, hi - lo)], ag_r.at[n])
+                for k in range(lo, hi):
+                    for h in range(2):
+                        block = dwv[8 * h : 8 * h + 8, k].reshape(HALF, HALF)
+                        part = lax.dot_general(small_eye, block, (((1,), (1,)), ((), ())), preferred_element_type=F32)
+                        dw_ref[core, k, h * HALF : (h + 1) * HALF, :] = part.astype(BF16)
+                hand_over(lo, hi, n).start()
+
+    for s in range(OWNERS):
         for h in range(2):
             @pl.when(jnp.logical_or(z4 != s, core != h))
             def _():
                 whole_wait(zs.at[s, h], z_s.at[2 * s + h])
 
-    @pl.when(z4 < GROUPS)
-    def _():
-        whole_wait(zgd, zg_s)
-        whole_wait(zgd, fin_s)
+    whole_wait(zgd, zg_s)
+    whole_wait(zgd, fin_s)
 
     whole_wait(xc.at[1, pl.ds(1, 15)], xa_s)
     whole_wait(gs.at[pl.ds(0, 15)], g_s)
@@ -510,33 +512,32 @@
         to_east.wait_send()
         sent_vertical(verticals[2:3])
 
-    for c in tails:
+    for s in range(OWNERS):
+        @pl.when(z4 == s)
+        def _():
+            for n, (lo, hi) in enumerate((FINAL[s],) + REST[s]):
+                whole_wait(dwv.at[pl.ds(0, 15), pl.ds(lo, hi - lo)], ag_s.at[n])
+                hand_over(lo, hi, n).wait()
+
+
+def finish(out_ref, ig_ref, dw_ref, out_hbm, ig_hbm, dw_hbm, wide, sems):
+    copies = [
+        pltpu.make_async_copy(out_ref, out_hbm, sems.at[K]),
+        pltpu.make_async_copy(ig_ref, ig_hbm, sems.at[K + 1]),
+    ]
+    for c in copies:
+        c.start()
+    for k in range(K):
+        for h in range(2):
+            wide[k, :, h * HALF : (h + 1) * HALF] = dw_ref[h, k].astype(F32)
+        copies.append(pltpu.make_async_copy(wide.at[k], dw_hbm.at[k], sems.at[k]))
+        copies[-1].start()
+    for c in copies:
         c.wait()
 
 
-def finish(out_ref, ig_ref, dw_ref, out_hbm, ig_hbm, dw_hbm, small, narrow, wide, sems):
-    loads = [pltpu.make_async_copy(dw_ref.at[k], narrow.at[k], sems.at[k]) for k in range(K)]
-    loads += [
-        pltpu.make_async_copy(out_ref, small.at[0], sems.at[K]),
-        pltpu.make_async_copy(ig_ref, small.at[1], sems.at[K + 1]),
-    ]
-    stores = [pltpu.make_async_copy(wide.at[k], dw_hbm.at[k], sems.at[K + 2 + k]) for k in range(K)]
-    stores += [
-        pltpu.make_async_copy(small.at[0], out_hbm, sems.at[2 * K + 2]),
-        pltpu.make_async_copy(small.at[1], ig_hbm, sems.at[2 * K + 3]),
-    ]
-    for c in loads:
-        c.start()
-    for k in range(K + 2):
-        loads[k].wait()
-        if k < K:
-            wide[k] = narrow[k].astype(F32)
-        stores[k].start()
-    for c in stores:
-        c.wait()
-
-
 def on_device(inputs, out_grad, weight, kernel_basis, band_start, band_width, lon_reach):
+    vmem = pl.BlockSpec(memory_space=pltpu.VMEM)
     hbm = pl.BlockSpec(memory_space=pltpu.HBM)
     dma = pltpu.SemaphoreType.DMA
     piece = (KG, SLICE, HALF)
@@ -565,30 +566,28 @@
         pltpu.VMEM((2, ROWS, COLS, CH), BF16),
         pltpu.VMEM((2, ROWS, COLS, CH), BF16),
         pltpu.VMEM((K * 2 * SLICE, HALF), F32),
-        pltpu.VMEM((GROUPS, 2) + piece, BF16),
+        pltpu.VMEM((OWNERS, 2) + piece, BF16),
         pltpu.VMEM((7,) + piece, BF16),
         pltpu.VMEM((4,) + piece, BF16),
         pltpu.VMEM((3,) + piece, BF16),
+        pltpu.VMEM((OWNERS,) + piece, BF16),
         pltpu.VMEM((K, SLICE, HALF), BF16),
         pltpu.VMEM((16, K, SLICE, HALF), BF16),
-        pltpu.VMEM((K, CH, HALF), BF16),
         pltpu.VMEM((16, 3, SLICE, CELLS), BF16),
         pltpu.VMEM((CH, CH), BF16),
-        pltpu.VMEM((ROWS, COLS, CH), BF16),
-        pltpu.VMEM((ROWS, COLS, CH), BF16),
         dma((8,)), dma((8,)), dma((8,)), dma, dma((3,)), dma((6,)), dma((6,)), dma((2,)), dma((2,)), dma, dma,
         dma((4,)), dma((4,)),
-        dma((6,)), dma, dma, dma, dma, dma((3,)), dma((2,)), dma((2,)), dma((2,)), dma((2,)), dma((2,)), dma, dma((4,)),
+        dma((8,)), dma, dma, dma, dma, dma((4,)), dma((3,)), dma((3,)), dma((3,)), dma((3,)), dma((2,)), dma,
     ]
     out, ig, dw = pl.pallas_call(
         kernel,
         out_shape=(
-            jax.ShapeDtypeStruct((ROWS, COLS, CH), BF16),
-            jax.ShapeDtypeStruct((ROWS, COLS, CH), BF16),
-            jax.ShapeDtypeStruct((K, CH, CH), BF16),
+            pltpu.VMEM((ROWS, COLS, CH), BF16),
+            pltpu.VMEM((ROWS, COLS, CH), BF16),
+            pltpu.VMEM((2, K, CH, HALF), BF16),
         ),
         in_specs=[hbm] * 7,
-        out_specs=(hbm, hbm, hbm),
+        out_specs=(vmem, vmem, vmem),
         scratch_shapes=scratch,
         compiler_params=pltpu.CompilerParams(collective_id=0, has_side_effects=True, vmem_limit_bytes=56 << 20),
     )(
@@ -602,15 +601,10 @@
             jax.ShapeDtypeStruct((ROWS, COLS, CH), BF16),
             jax.ShapeDtypeStruct((K, CH, CH), F32),
         ),
-        in_specs=[hbm] * 3,
+        in_specs=[vmem] * 3,
         out_specs=(hbm, hbm, hbm),
-        scratch_shapes=[
-            pltpu.VMEM((2, ROWS, COLS, CH), BF16),
-            pltpu.VMEM((K, CH, CH), BF16),
-            pltpu.VMEM((K, CH, CH), F32),
-            dma((2 * K + 4,)),
-        ],
-        compiler_params=pltpu.CompilerParams(vmem_limit_bytes=56 << 20),
+        scratch_shapes=[pltpu.VMEM((K, CH, CH), F32), dma((K + 2,))],
+        compiler_params=pltpu.CompilerParams(vmem_limit_bytes=8 << 20),
     )(out, ig, dw)
 
 

time: 63 us -> 60.9 us (0.967)
  Pallas kernels: 61.9 us -> 60.1 us
    pallas_call x1, Pallas kernels: 2.54 us -> 1.53 us  [on_device(): pl.pallas_call(finish, out_shape=(jax.ShapeDtypeStruct((ROWS, COLS, CH),...]
    pallas_call x1, Pallas kernels: 59.4 us -> 58.5 us  [on_device(): pl.pallas_call(kernel, out_shape=(pltpu.VMEM((ROWS, COLS, CH), BF16), plt...]
where the time goes in v5:
time: 60.9 us; the launch traced here: 60.7 us
  Pallas kernels  60.1 us (99%)
  between operations  0.64 us (1%)
    pallas_call x1, Pallas kernels, on_device(): pl.pallas_call(kernel, out_shape=(pltpu.VMEM((ROWS, COLS, CH), BF16), plt...  58.5 us
    pallas_call x1, Pallas kernels, on_device(): pl.pallas_call(finish, out_shape=(jax.ShapeDtypeStruct((ROWS, COLS, CH),...  1.53 us

profile of v5, /device:TPU:1, one launch (start us, length us, event | category | flops | bytes accessed | tf_op | source)
XLA Modules:
  0.0 60.7 jit_solution(16127899353602764957)
XLA Ops:
  0.6 58.5 %shard_map.94 = (bf16[8,16,256]{2,1,0:T(8,128)(2,1)S(1)}, bf16[8,16,256]{2,1,0:T(8,128)(2,1)S(1)}, bf16[2,9,256,128]{3,2,1,0:T(8,128)(2,1)S(1)}) custom-call(bf16[8,16,256]{2,1,0:T(8,128)(2,1)} %x_ref.1, bf16[128,256]{1,0:T(8,128)(2,1)} %bitcast.3, bf16[9,256,256]{2,1,0:T(8,128)(2,1)} %w_ref.1, bf16[9,17,8,33]{3,2,1,0:T(8,128)(2,1)} %bitcast.2, s32[8]{0:T(128)} %start_ref.1, ...), custom_call_target="tpu_custom_call" | custom-call | tf_op jit(solution)/shard_map/pallas_call | solution.py:582
  59.2 1.5 %shard_map.95 = (bf16[8,16,256]{2,1,0:T(8,128)(2,1)}, bf16[8,16,256]{2,1,0:T(8,128)(2,1)}, f32[9,256,256]{2,1,0:T(8,128)}) custom-call(bf16[8,16,256]{2,1,0:T(8,128)(2,1)S(1)} %get-tuple-element.6.out_ref, bf16[8,16,256]{2,1,0:T(8,128)(2,1)S(1)} %get-tuple-element.7.ig_ref, bf16[2,9,256,128]{3,2,1,0:T(8,128)(2,1)S(1)} %get-tuple-element.8.dw_ref), custom_call_target="tpu_custom_call" | custom-call | tf_op jit(solution)/shard_map/pallas_call | solution.py:597
